TPU v7x, 256 devices: a whole 4x4x8 slice. The times are simulated.
256 devices in a mesh: frames: 128 (over y, z_hi, x, core), strip: 2 (over z_lo).
Axes of the slice: x: 4, y: 4, z: 8 (z_hi: 4, z_lo: 2; z = z_hi * 2 + z_lo), core: 2. Of those that a mesh axis runs over, the one named last changes fastest.
Arguments:
- queries: bfloat16 [65536, 1024], P(('frames', 'strip')), may hold values from -16 to 16
- keys: bfloat16 [65536, 1024], P(('frames', 'strip')), may hold values from -16 to 16
- values: bfloat16 [65536, 1024], P(('frames', 'strip')), may hold values from -6 to 6
- out_grad: bfloat16 [65536, 1024], P(('frames', 'strip')), may hold values from -6 to 6
- block_list: int32 [1024, 13], P(('frames', 'strip')), may hold values from 0 to 23, as said below
- block_count: int32 [1024], P(('frames', 'strip')), may hold values from 1 to 13
Outputs:
- attended: bfloat16 [65536, 1024], P(('frames', 'strip'))
- query_grad: bfloat16 [65536, 1024], P(('frames', 'strip'))
- key_grad: bfloat16 [65536, 1024], P(('frames', 'strip'))
- value_grad: bfloat16 [65536, 1024], P(('frames', 'strip'))
Inputs may be any that keep to these rules, and one draw needn't show every extreme that they name: `block_list`: each row holds 13 different window block numbers; its first entry is 8 + (b mod (8)), the query block's own block.
All inputs are finite; a program needn't handle non-finite values.
Results may differ from a plain program's by a relative error of at most 0.025.
Values may be sent and summed in bfloat16 or wider, within the bound.
A program may use at most 128 MiB of HBM per device.

v0:
```python
import jax
import jax.numpy as jnp
from jax import lax
from jax.experimental import pallas as pl
from jax.experimental.pallas import tpu as pltpu
from jax.sharding import PartitionSpec as P

HD = 64
BLOCK = 64
SEL = 13
HALF = 4
FRAME = 8
WINDOW = 24
GROUPS = 4
LANES = 128
FACTOR = 0.125
MASKED = -1e30
PLACE_AT = 32
RUN = 8
MESH = pl.DeviceIdType.MESH


def kernel(
    frames,
    block_list, block_count, queries, keys, values, out_grad,
    attended, query_grad, key_grad, value_grad,
    loaded, packed, kv, qd, work, tiles, rows_out, rows_in, give, take, own, final, final_in, relay, meta_vm, meta_sm,
    load_sem, in_send, in_recv, pass_send, pass_recv,
    meta_send, meta_recv, meta_local, row_send, row_recv, row_local,
    term_send, term_recv, grad_send, grad_recv, grad_local, relay_send, relay_recv,
):
    f, s = lax.axis_index("frames"), lax.axis_index("strip")
    o = 1 - s
    after, before = lax.rem(f + 1, frames), lax.rem(f + frames - 1, frames)
    partner, next_dev, prev_dev = (f, o), (after, s), (before, s)

    sources = (keys, values, queries, out_grad)
    loads = [pltpu.make_async_copy(sources[a], loaded.at[a], load_sem.at[a]) for a in range(4)]
    for load in loads:
        load.start()

    place_in_run = lax.rem(f, RUN)
    edge = (place_in_run == RUN - 1, place_in_run == 0)
    part_column = (3 * s, 1 + s)

    def relay_of(d, column):
        if d == 0:
            return (lax.rem(f + 1 + 2 * column, frames), s)
        return (lax.rem(f + frames - 1 - 2 * column, frames), s)

    relay_back = lax.rem(place_in_run, 2)
    relay_column = lax.select(relay_back == 0, place_in_run // 2, (RUN - 1 - place_in_run) // 2)
    is_relay = ((relay_column == 1) & (s == 0)) | ((relay_column >= 2) & (s == 1))
    relay_half = lax.rem(relay_column, 2)
    relay_target_frame = f - place_in_run + relay_back * (RUN - 1)
    relay_source_frame = lax.rem(relay_target_frame + frames - 1 + 2 * relay_back, frames)
    relay_target, relay_source = (relay_target_frame, s), (relay_source_frame, s)

    def relay_in_run(d, column):
        return f - 2 * column if d == 0 else f + 2 * column

    barrier = pltpu.get_barrier_semaphore()

    def greet(device):
        pl.semaphore_signal(barrier, inc=1, device_id=device, device_id_type=MESH)

    for device in (partner, next_dev, prev_dev):
        greet(device)

    @pl.when(is_relay)
    def _():
        greet(relay_source)
        greet(relay_target)

    for d in range(2):
        for column in (1, 2, 3):
            @pl.when(edge[d] & (s == (0 if column == 1 else 1)))
            def _():
                greet(relay_of(d, column))
                greet((relay_in_run(d, column), s))

    at_end = (edge[0] | edge[1]).astype(jnp.int32)
    pl.semaphore_wait(barrier, 3 + 2 * is_relay.astype(jnp.int32) + at_end * (2 + 2 * s))

    def remote(src, dst, send, recv, device):
        return pltpu.make_async_remote_copy(
            src_ref=src, dst_ref=dst, send_sem=send, recv_sem=recv,
            device_id=device, device_id_type=MESH,
        )

    def columns(half, g):
        return pl.ds(pl.multiple_of(half * (GROUPS * LANES) + g * LANES, LANES), LANES)

    def landing(g, pair, half):
        if pair == 0:
            return kv.at[g, pl.ds(FRAME + HALF * half, HALF)]
        return qd.at[g, pl.ds(HALF * half, HALF)]

    def swap(g, pair):
        return remote(
            packed.at[g, pair], landing(g, pair, s), in_send.at[g, pair], in_recv.at[g, pair], partner
        )

    def pack(g, pair):
        for a in range(2):
            lanes = slice(a * LANES, (a + 1) * LANES)
            packed[g, pair, :, :, lanes] = loaded[2 * pair + a, :, :, columns(o, g)]

    def keep(g, pair):
        own_rows = landing(g, pair, s)
        for a in range(2):
            lanes = slice(a * LANES, (a + 1) * LANES)
            own_rows[:, :, lanes] = loaded[2 * pair + a, :, :, columns(s, g)]

    neighbours = (next_dev, prev_dev)

    def start_part(d, part, src, dst, send, recv, phase, g):
        straight = remote(src, dst, send, recv, neighbours[d])
        if part == 0:
            bent = edge[d] & (s == 1)
        else:
            bent = edge[d]

        @pl.when(bent)
        def _():
            remote(
                src, relay.at[phase, g], send, relay_recv.at[phase, g], relay_of(d, part_column[part])
            ).start()

        @pl.when(jnp.logical_not(bent))
        def _():
            straight.start()

    def kv_window(g, base, half):
        return kv.at[g, pl.ds(base + HALF * half, HALF)]

    def pass_args(g, d, part):
        half = (s, o)[part]
        return (
            kv_window(g, FRAME, half), kv_window(g, (0, 2 * FRAME)[d], half),
            pass_send.at[g, d, half], pass_recv.at[g, d, half],
        )

    def start_pass(g, d, part):
        start_part(d, part, *pass_args(g, d, part), 0, g)

    def wait_pass(g, d, part):
        return remote(*pass_args(g, d, part), neighbours[d])

    def term_args(g, d, part):
        half = (s, o)[part]
        at = pl.ds(HALF * half, HALF)
        return (
            give.at[g, d, at], take.at[g, d, at], term_send.at[g, d, half], term_recv.at[g, d, half]
        )

    def start_terms(g, d, part):
        start_part(d, part, *term_args(g, d, part), 1, g)

    def wait_terms(g, d, part):
        return remote(*term_args(g, d, part), neighbours[d])

    def relay_on(g, phase):
        if phase == 0:
            target = kv_window(g, relay_back * (2 * FRAME), relay_half)
            recv = pass_recv.at[g, relay_back, relay_half]
        else:
            target = take.at[g, relay_back, pl.ds(HALF * relay_half, HALF)]
            recv = term_recv.at[g, relay_back, relay_half]
        return remote(relay.at[phase, g], target, relay_send.at[phase, g], recv, relay_target)

    def relay_step(g, phase):
        @pl.when(is_relay)
        def _():
            remote(
                relay.at[phase, g], relay.at[phase, g], relay_send.at[phase, g],
                relay_recv.at[phase, g], relay_target,
            ).wait_recv()
            relay_on(g, phase).start()

    def rows_across(g):
        return remote(
            rows_out.at[g, pl.ds(HALF * o, HALF)], rows_in.at[g], row_send.at[g], row_recv.at[g], partner
        )

    def grads_across(g):
        return remote(
            final.at[g, pl.ds(HALF * o, HALF)], final_in.at[g], grad_send.at[g], grad_recv.at[g], partner
        )

    row_targets, grad_targets = (query_grad, attended), (key_grad, value_grad)

    def place_copy(staged, targets, local, g, half, a):
        return pltpu.make_async_copy(
            staged.at[:, :, pl.ds(a * LANES, LANES)], targets[a].at[:, :, columns(half, g)], local.at[g, a]
        )

    def rows_along(g, a):
        return place_copy(rows_out.at[g, pl.ds(HALF * s, HALF)], row_targets, row_local, g, s, a)

    def grads_along(g, a):
        return place_copy(final.at[g, pl.ds(HALF * s, HALF)], grad_targets, grad_local, g, s, a)

    def rows_back(g, a):
        return place_copy(rows_in.at[g], row_targets, row_local.at[pl.ds(GROUPS, GROUPS)], g, o, a)

    def grads_back(g, a):
        return place_copy(final_in.at[g], grad_targets, grad_local.at[pl.ds(GROUPS, GROUPS)], g, o, a)

    share_meta = remote(meta_vm.at[s], meta_vm.at[s], meta_send, meta_recv, partner)

    def begin(g):
        for pair in range(2):
            pack(g, pair)
            swap(g, pair).start()

    def begin_own(g):
        keep(g, 0)
        for d in range(2):
            start_pass(g, d, 0)
        keep(g, 1)

    for load in loads:
        load.wait()
    begin(0)
    begin_own(0)
    begin(1)
    begin_own(1)

    listed = block_list[...]
    row_at = lax.broadcasted_iota(jnp.int32, (HALF, LANES), 0)
    lane_at = lax.broadcasted_iota(jnp.int32, (HALF, LANES), 1)
    counts = jnp.zeros((HALF, LANES), jnp.int32)
    for row in range(HALF):
        counts = jnp.where(row_at == row, block_count[row], counts)
    edge_low = jnp.where(f > 0, 0, FRAME)
    edge_high = jnp.where(f < frames - 1, WINDOW, 2 * FRAME)
    usable = (listed >= edge_low) & (listed < edge_high) & (lane_at[:, :SEL] < counts[:, :SEL])
    slots = jnp.where(usable, listed, -1)
    place = jnp.full((HALF, LANES), SEL, jnp.int32)
    for j in range(SEL):
        place = jnp.where(lane_at - PLACE_AT == slots[:, j:j + 1], j, place)
    meta_vm[s, 0:HALF] = place
    meta_vm[s, 0:HALF, 0:SEL] = listed
    meta_vm[s, HALF:] = jnp.zeros((HALF, LANES), jnp.int32)
    meta_vm[s, HALF:, 0:SEL] = usable.astype(jnp.int32)
    share_meta.start()
    share_meta.wait()
    to_scalar = pltpu.make_async_copy(meta_vm, meta_sm, meta_local)
    to_scalar.start()
    to_scalar.wait()

    tiles[:, SEL] = jnp.zeros((FRAME, BLOCK, 2 * LANES), jnp.float32)

    def forward(g):
        swap(g, 0).wait_recv()
        for d in range(2):
            start_pass(g, d, 1)

    forward(0)
    begin(2)
    begin_own(2)
    relay_step(0, 0)
    forward(1)

    row_ids = lax.broadcasted_iota(jnp.int32, (4 * HD, 4 * HD), 0) // HD
    col_ids = lax.broadcasted_iota(jnp.int32, (4 * HD, 4 * HD), 1) // HD
    spread = jnp.where(
        row_ids == col_ids, jnp.where(col_ids < 2, FACTOR, 1.0), 0.0
    ).astype(jnp.bfloat16)
    first_head = lax.broadcasted_iota(jnp.int32, (BLOCK, LANES), 1) < HD

    def heads(full):
        return jnp.where(first_head, full[:HD], full[HD:])

    def fold(array, op):
        return op(array.reshape(array.shape[0] // 8, 8, LANES), axis=0)

    def attend(g, b):
        strip, row = b // HALF, lax.rem(b, HALF)
        part = qd[g, b]
        diagonal = jnp.concatenate([part] * 4, axis=0) * spread
        picked = jnp.concatenate(
            [work[meta_sm[strip, row, j]] for j in range(SEL)], axis=0
        )
        both = lax.dot_general(
            picked, diagonal, (((1,), (1,)), ((), ())), preferred_element_type=jnp.float32
        )
        bias = [
            jnp.where(meta_sm[strip, HALF + row, j] > 0, 0.0, MASKED).astype(jnp.float32)
            for j in range(SEL)
        ]
        parts = [both[j * BLOCK:(j + 1) * BLOCK, :LANES] for j in range(SEL)]
        peak = fold(parts[0], jnp.max) + bias[0]
        for j in range(1, SEL):
            peak = jnp.maximum(peak, fold(parts[j], jnp.max) + bias[j])
        peak = jnp.max(peak, axis=0, keepdims=True)
        powers = [jnp.exp(parts[j] - (peak - bias[j])) for j in range(SEL)]
        grad_weights = [both[j * BLOCK:(j + 1) * BLOCK, LANES:] for j in range(SEL)]
        total = fold(powers[0], jnp.sum)
        dots = fold(powers[0] * grad_weights[0], jnp.sum)
        for j in range(1, SEL):
            total = total + fold(powers[j], jnp.sum)
            dots = dots + fold(powers[j] * grad_weights[j], jnp.sum)
        scale = 1.0 / jnp.sum(total, axis=0, keepdims=True)
        row_dots = jnp.sum(dots, axis=0, keepdims=True) * scale
        slabs = []
        for j in range(SEL):
            weights = powers[j] * scale
            grad_scores = weights * (grad_weights[j] - row_dots)
            slabs.append(jnp.concatenate([grad_scores, weights], axis=1).astype(jnp.bfloat16))
        slab = jnp.concatenate(slabs, axis=0)
        terms = jnp.dot(slab, diagonal, preferred_element_type=jnp.float32)
        tiles[b, :SEL] = terms.reshape(SEL, BLOCK, 2 * LANES)
        mixed = lax.dot_general(
            slab, picked, (((0,), (0,)), ((), ())), preferred_element_type=jnp.float32
        )
        rows_out[g, b] = jnp.concatenate(
            [heads(mixed[:LANES, :LANES]) * FACTOR, heads(mixed[LANES:, LANES:])], axis=1
        ).astype(jnp.bfloat16)

    def finish(g):
        slot = lax.rem(g, 2)
        for d in range(2):
            for part in range(2):
                wait_terms(g, d, part).wait_recv()

        def add(w, carry):
            total = own[slot, w] + take[g, 0, w].astype(jnp.float32) + take[g, 1, w].astype(jnp.float32)
            final[g, w] = total.astype(jnp.bfloat16)
            return carry

        lax.fori_loop(0, FRAME, add, 0)
        grads_across(g).start()
        for a in range(2):
            grads_along(g, a).start()

    def one_group(g, carry):
        swap(g, 1).wait_recv()
        for d in range(2):
            for part in range(2):
                wait_pass(g, d, part).wait_recv()

        @pl.when(g + 3 < GROUPS)
        def _():
            begin(g + 3)
            begin_own(g + 3)

        work[...] = kv[g]

        def two_blocks(i, inner):
            b = lax.rem(HALF * o + 2 * i, FRAME)
            attend(g, b)
            attend(g, b + 1)

            @pl.when((i == 0) & (g > 1))
            def _():
                finish(g - 2)

            @pl.when((i == 0) & (g == 0))
            def _():
                relay_step(1, 0)

            @pl.when(i == 1)
            def _():
                rows_across(g).start()

                @pl.when(g + 2 < GROUPS)
                def _():
                    forward(g + 2)

            @pl.when((i == 2) & (g > 0))
            def _():
                relay_step(g - 1, 1)

            @pl.when((i == 3) & (g + 2 < GROUPS))
            def _():
                relay_step(g + 2, 0)

            return inner

        lax.fori_loop(0, FRAME // 2, two_blocks, 0)
        for a in range(2):
            rows_along(g, a).start()

        def gather(w, base):
            acc = None
            for b in range(FRAME):
                place = meta_sm[b // HALF, b % HALF, PLACE_AT + base + w]
                tile = tiles[b, place]
                acc = tile if acc is None else acc + tile
            return acc

        def collect(w, inner):
            give[g, 1, w] = gather(w, 0).astype(jnp.bfloat16)
            give[g, 0, w] = gather(w, 2 * FRAME).astype(jnp.bfloat16)
            return inner

        lax.fori_loop(0, FRAME, collect, 0)
        for d in range(2):
            for part in range(2):
                start_terms(g, d, part)

        def collect_own(w, inner):
            own[lax.rem(g, 2), w] = gather(w, FRAME)
            return inner

        lax.fori_loop(0, FRAME, collect_own, 0)

        return carry

    lax.fori_loop(0, GROUPS, one_group, 0)
    finish(GROUPS - 2)
    relay_step(GROUPS - 1, 1)
    finish(GROUPS - 1)

    def land(g, carry):
        rows_across(g).wait_recv()
        for a in range(2):
            rows_back(g, a).start()
        grads_across(g).wait_recv()
        for a in range(2):
            grads_back(g, a).start()
        return carry

    lax.fori_loop(0, GROUPS, land, 0)

    def drain(g, carry):
        for pair in range(2):
            swap(g, pair).wait_send()
        for d in range(2):
            for part in range(2):
                wait_pass(g, d, part).wait_send()
                wait_terms(g, d, part).wait_send()

        @pl.when(is_relay)
        def _():
            for phase in range(2):
                relay_on(g, phase).wait_send()

        rows_across(g).wait_send()
        grads_across(g).wait_send()
        for a in range(2):
            rows_along(g, a).wait()
            grads_along(g, a).wait()
            rows_back(g, a).wait()
            grads_back(g, a).wait()
        return carry

    lax.fori_loop(0, GROUPS, drain, 0)


def hand_over(*refs):
    sources, targets, sems = refs[:4], refs[4:8], refs[8]
    copies = [
        pltpu.make_async_copy(src.at[pl.ds(at * 2, 2)], dst.at[pl.ds(at * 2, 2)], sems.at[i, at])
        for i, (src, dst) in enumerate(zip(sources, targets))
        for at in range(2)
    ]
    for copy in copies:
        copy.start()
    for copy in copies:
        copy.wait()


def body(queries, keys, values, out_grad, block_list, block_count):
    rows, width = queries.shape
    frames = lax.axis_size("frames")
    blocked = [x.reshape(HALF, BLOCK, width) for x in (queries, keys, values, out_grad)]
    shape = jax.ShapeDtypeStruct((HALF, BLOCK, width), jnp.bfloat16)
    dma = pltpu.SemaphoreType.DMA
    flops = 6 * 2 * FRAME * SEL * BLOCK * 256 * 256 * GROUPS
    outs = pl.pallas_call(
        lambda *refs: kernel(frames, *refs),
        out_shape=[shape] * 4,
        in_specs=[pl.BlockSpec(memory_space=pltpu.VMEM), pl.BlockSpec(memory_space=pltpu.SMEM)] + [pl.BlockSpec(memory_space=pl.ANY)] * 4,
        out_specs=[pl.BlockSpec(memory_space=pl.ANY)] * 4,
        scratch_shapes=[
            pltpu.VMEM((4, HALF, BLOCK, width), jnp.bfloat16),
            pltpu.VMEM((GROUPS, 2, HALF, BLOCK, 2 * LANES), jnp.bfloat16),
            pltpu.VMEM((GROUPS, WINDOW, BLOCK, 2 * LANES), jnp.bfloat16),
            pltpu.VMEM((GROUPS, FRAME, BLOCK, 2 * LANES), jnp.bfloat16),
            pltpu.VMEM((WINDOW, BLOCK, 2 * LANES), jnp.bfloat16),
            pltpu.VMEM((FRAME, SEL + 1, BLOCK, 2 * LANES), jnp.float32),
            pltpu.VMEM((GROUPS, FRAME, BLOCK, 2 * LANES), jnp.bfloat16),
            pltpu.VMEM((GROUPS, HALF, BLOCK, 2 * LANES), jnp.bfloat16),
            pltpu.VMEM((GROUPS, 2, FRAME, BLOCK, 2 * LANES), jnp.bfloat16),
            pltpu.VMEM((GROUPS, 2, FRAME, BLOCK, 2 * LANES), jnp.bfloat16),
            pltpu.VMEM((2, FRAME, BLOCK, 2 * LANES), jnp.float32),
            pltpu.VMEM((GROUPS, FRAME, BLOCK, 2 * LANES), jnp.bfloat16),
            pltpu.VMEM((GROUPS, HALF, BLOCK, 2 * LANES), jnp.bfloat16),
            pltpu.VMEM((2, GROUPS, HALF, BLOCK, 2 * LANES), jnp.bfloat16),
            pltpu.VMEM((2, 8, LANES), jnp.int32),
            pltpu.SMEM((2, 8, LANES), jnp.int32),
            dma((4,)), dma((GROUPS, 2)), dma((GROUPS, 2)),
            dma((GROUPS, 2, 2)), dma((GROUPS, 2, 2)),
            dma, dma, dma,
            dma((GROUPS,)), dma((GROUPS,)), dma((2 * GROUPS, 2)),
            dma((GROUPS, 2, 2)), dma((GROUPS, 2, 2)),
            dma((GROUPS,)), dma((GROUPS,)), dma((2 * GROUPS, 2)),
            dma((2, GROUPS)), dma((2, GROUPS)),
        ],
        cost_estimate=pl.CostEstimate(
            flops=flops, bytes_accessed=16 * rows * width, transcendentals=FRAME * SEL * BLOCK * LANES * GROUPS
        ),
        compiler_params=pltpu.CompilerParams(
            collective_id=0, has_side_effects=True, vmem_limit_bytes=60 * 1024 * 1024
        ),
    )(block_list, block_count, *blocked)
    outs = pl.pallas_call(
        hand_over,
        out_shape=[shape] * 4,
        in_specs=[pl.BlockSpec(memory_space=pltpu.VMEM)] * 4,
        out_specs=[pl.BlockSpec(memory_space=pl.ANY)] * 4,
        scratch_shapes=[dma((4, 2))],
        compiler_params=pltpu.CompilerParams(vmem_limit_bytes=60 * 1024 * 1024),
    )(*outs)
    return tuple(x.reshape(rows, width) for x in outs)


def solution(mesh):
    split = P(("frames", "strip"), None)
    in_specs = (split, split, split, split, split, P(("frames", "strip")))
    return jax.shard_map(
        body, mesh=mesh, in_specs=in_specs, out_specs=(split,) * 4, check_vma=False
    )
```

profile of v0, /device:TPU:32, one launch (start us, length us, event | category | flops | bytes accessed | tf_op | source)
XLA Modules:
  0.0 112.5 jit_solution(9933586765429387128)
XLA Ops:
  0.6 108.9 %shard_map.93 = (bf16[4,64,1024]{2,1,0:T(8,128)(2,1)}, bf16[4,64,1024]{2,1,0:T(8,128)(2,1)}, bf16[4,64,1024]{2,1,0:T(8,128)(2,1)}, bf16[4,64,1024]{2,1,0:T(8,128)(2,1)}) custom-call(s32[4,13]{1,0:T(4,128)} %refs_0_.1, s32[4]{0:T(128)} %refs_1_.1, bf16[4,64,1024]{2,1,0:T(8,128)(2,1)} %bitcast.8, bf16[4,64,1024]{2,1,0:T(8,128)(2,1)} %bitcast.9, ...), custom_call_target="tpu_custom_call" | custom-call | flops 20937965568 | bytes 4194304 | tf_op jit(solution)/shard_map/pallas_call | solution.py:473
  109.6 2.9 %shard_map.94 = (bf16[4,64,1024]{2,1,0:T(8,128)(2,1)}, bf16[4,64,1024]{2,1,0:T(8,128)(2,1)}, bf16[4,64,1024]{2,1,0:T(8,128)(2,1)}, bf16[4,64,1024]{2,1,0:T(8,128)(2,1)}) custom-call(bf16[4,64,1024]{2,1,0:T(8,128)(2,1)} %get-tuple-element.12.refs_0_, bf16[4,64,1024]{2,1,0:T(8,128)(2,1)} %get-tuple-element.13.refs_1_, ...), custom_call_target="tpu_custom_call" | custom-call | tf_op jit(solution)/shard_map/pallas_call | solution.py:510
where the time goes:
time: 113 us; the launch traced here: 112 us
  Pallas kernels  112 us (99%)
    pallas_call x1, Pallas kernels, body(): pl.pallas_call(lambda *refs: kernel(frames, *refs), out_shape=[shape] * 4...  109 us
    pallas_call x1, Pallas kernels, body(): pl.pallas_call(hand_over, out_shape=[shape] * 4, in_specs=[pl.BlockSpec(m...  2.89 us

commit v1 on v0

--- a/solution.py
+++ b/solution.py
@@ -44,20 +44,20 @@
     part_column = (3 * s, 1 + s)
 
     def relay_of(d, column):
+        return (f - 2 * column if d == 0 else f + 2 * column, s)
+
+    def relay_to(d, column):
         if d == 0:
             return (lax.rem(f + 1 + 2 * column, frames), s)
         return (lax.rem(f + frames - 1 - 2 * column, frames), s)
 
-    relay_back = lax.rem(place_in_run, 2)
-    relay_column = lax.select(relay_back == 0, place_in_run // 2, (RUN - 1 - place_in_run) // 2)
+    relay_back = 1 - lax.rem(place_in_run, 2)
+    relay_column = lax.select(relay_back == 0, (RUN - 1 - place_in_run) // 2, place_in_run // 2)
     is_relay = ((relay_column == 1) & (s == 0)) | ((relay_column >= 2) & (s == 1))
     relay_half = lax.rem(relay_column, 2)
-    relay_target_frame = f - place_in_run + relay_back * (RUN - 1)
-    relay_source_frame = lax.rem(relay_target_frame + frames - 1 + 2 * relay_back, frames)
+    relay_source_frame = f - place_in_run + (1 - relay_back) * (RUN - 1)
+    relay_target_frame = lax.rem(relay_source_frame + frames + 1 - 2 * relay_back, frames)
     relay_target, relay_source = (relay_target_frame, s), (relay_source_frame, s)
-
-    def relay_in_run(d, column):
-        return f - 2 * column if d == 0 else f + 2 * column
 
     barrier = pltpu.get_barrier_semaphore()
 
@@ -77,7 +77,7 @@
             @pl.when(edge[d] & (s == (0 if column == 1 else 1)))
             def _():
                 greet(relay_of(d, column))
-                greet((relay_in_run(d, column), s))
+                greet(relay_to(d, column))
 
     at_end = (edge[0] | edge[1]).astype(jnp.int32)
     pl.semaphore_wait(barrier, 3 + 2 * is_relay.astype(jnp.int32) + at_end * (2 + 2 * s))

time: 113 us -> 90.7 us (0.80)
  the two profiles are of different devices: /device:TPU:32 before, /device:TPU:0 now
where the time goes in v1:
time: 90.7 us; the launch traced here: 90.6 us
  Pallas kernels  89.9 us (99%)
    pallas_call x1, Pallas kernels, body(): pl.pallas_call(lambda *refs: kernel(frames, *refs), out_shape=[shape] * 4...  87 us
    pallas_call x1, Pallas kernels, body(): pl.pallas_call(hand_over, out_shape=[shape] * 4, in_specs=[pl.BlockSpec(m...  2.89 us

profile of v1, /device:TPU:0, one launch (start us, length us, event | category | flops | bytes accessed | tf_op | source)
XLA Modules:
  0.0 90.6 jit_solution(9514154392025770403)
XLA Ops:
  0.6 87.0 %shard_map.93 = (bf16[4,64,1024]{2,1,0:T(8,128)(2,1)}, bf16[4,64,1024]{2,1,0:T(8,128)(2,1)}, bf16[4,64,1024]{2,1,0:T(8,128)(2,1)}, bf16[4,64,1024]{2,1,0:T(8,128)(2,1)}) custom-call(s32[4,13]{1,0:T(4,128)} %refs_0_.1, s32[4]{0:T(128)} %refs_1_.1, bf16[4,64,1024]{2,1,0:T(8,128)(2,1)} %bitcast.8, bf16[4,64,1024]{2,1,0:T(8,128)(2,1)} %bitcast.9, ...), custom_call_target="tpu_custom_call" | custom-call | flops 20937965568 | bytes 4194304 | tf_op jit(solution)/shard_map/pallas_call | solution.py:473
  87.7 2.9 %shard_map.94 = (bf16[4,64,1024]{2,1,0:T(8,128)(2,1)}, bf16[4,64,1024]{2,1,0:T(8,128)(2,1)}, bf16[4,64,1024]{2,1,0:T(8,128)(2,1)}, bf16[4,64,1024]{2,1,0:T(8,128)(2,1)}) custom-call(bf16[4,64,1024]{2,1,0:T(8,128)(2,1)} %get-tuple-element.12.refs_0_, bf16[4,64,1024]{2,1,0:T(8,128)(2,1)} %get-tuple-element.13.refs_1_, ...), custom_call_target="tpu_custom_call" | custom-call | tf_op jit(solution)/shard_map/pallas_call | solution.py:510

commit v2 on v1

--- a/solution.py
+++ b/solution.py
@@ -220,12 +220,15 @@
             start_pass(g, d, 0)
         keep(g, 1)
 
-    for load in loads:
-        load.wait()
-    begin(0)
-    begin_own(0)
-    begin(1)
-    begin_own(1)
+    for pair in range(2):
+        loads[2 * pair].wait()
+        loads[2 * pair + 1].wait()
+        pack(0, pair)
+        swap(0, pair).start()
+        keep(0, pair)
+        if pair == 0:
+            for d in range(2):
+                start_pass(0, d, 0)
 
     listed = block_list[...]
     row_at = lax.broadcasted_iota(jnp.int32, (HALF, LANES), 0)
@@ -245,11 +248,8 @@
     meta_vm[s, HALF:] = jnp.zeros((HALF, LANES), jnp.int32)
     meta_vm[s, HALF:, 0:SEL] = usable.astype(jnp.int32)
     share_meta.start()
-    share_meta.wait()
-    to_scalar = pltpu.make_async_copy(meta_vm, meta_sm, meta_local)
-    to_scalar.start()
-    to_scalar.wait()
-
+    begin(1)
+    begin_own(1)
     tiles[:, SEL] = jnp.zeros((FRAME, BLOCK, 2 * LANES), jnp.float32)
 
     def forward(g):
@@ -258,9 +258,13 @@
             start_pass(g, d, 1)
 
     forward(0)
+    share_meta.wait()
+    to_scalar = pltpu.make_async_copy(meta_vm, meta_sm, meta_local)
+    to_scalar.start()
+    relay_step(0, 0)
     begin(2)
     begin_own(2)
-    relay_step(0, 0)
+    to_scalar.wait()
     forward(1)
 
     row_ids = lax.broadcasted_iota(jnp.int32, (4 * HD, 4 * HD), 0) // HD
@@ -334,6 +338,9 @@
         grads_across(g).start()
         for a in range(2):
             grads_along(g, a).start()
+        rows_across(g).wait_recv()
+        for a in range(2):
+            rows_back(g, a).start()
 
     def one_group(g, carry):
         swap(g, 1).wait_recv()
@@ -348,38 +355,38 @@
 
         work[...] = kv[g]
 
-        def two_blocks(i, inner):
-            b = lax.rem(HALF * o + 2 * i, FRAME)
-            attend(g, b)
-            attend(g, b + 1)
+        def four_blocks(i, inner):
+            first = lax.rem(HALF * o + HALF * i, FRAME)
+            for b in range(HALF):
+                attend(g, first + b)
 
             @pl.when((i == 0) & (g > 1))
             def _():
                 finish(g - 2)
 
+            @pl.when(i == 0)
+            def _():
+                rows_across(g).start()
+
+                @pl.when(g + 2 < GROUPS)
+                def _():
+                    forward(g + 2)
+
             @pl.when((i == 0) & (g == 0))
             def _():
                 relay_step(1, 0)
 
-            @pl.when(i == 1)
-            def _():
-                rows_across(g).start()
-
-                @pl.when(g + 2 < GROUPS)
-                def _():
-                    forward(g + 2)
-
-            @pl.when((i == 2) & (g > 0))
+            @pl.when((i == 0) & (g > 0))
             def _():
                 relay_step(g - 1, 1)
 
-            @pl.when((i == 3) & (g + 2 < GROUPS))
+            @pl.when((i == 1) & (g + 2 < GROUPS))
             def _():
                 relay_step(g + 2, 0)
 
             return inner
 
-        lax.fori_loop(0, FRAME // 2, two_blocks, 0)
+        lax.fori_loop(0, 2, four_blocks, 0)
         for a in range(2):
             rows_along(g, a).start()
 
@@ -415,9 +422,6 @@
     finish(GROUPS - 1)
 
     def land(g, carry):
-        rows_across(g).wait_recv()
-        for a in range(2):
-            rows_back(g, a).start()
         grads_across(g).wait_recv()
         for a in range(2):
             grads_back(g, a).start()
@@ -451,15 +455,16 @@
 
 
 def hand_over(*refs):
-    sources, targets, sems = refs[:4], refs[4:8], refs[8]
-    copies = [
-        pltpu.make_async_copy(src.at[pl.ds(at * 2, 2)], dst.at[pl.ds(at * 2, 2)], sems.at[i, at])
-        for i, (src, dst) in enumerate(zip(sources, targets))
-        for at in range(2)
-    ]
-    for copy in copies:
+    sources, targets, held, in_sems, out_sems = refs[:4], refs[4:8], refs[8], refs[9], refs[10]
+    spots = [(i, at) for i in range(4) for at in range(HALF)]
+    ins = [pltpu.make_async_copy(sources[i].at[at], held.at[i, at], in_sems.at[i, at]) for i, at in spots]
+    outs = [pltpu.make_async_copy(held.at[i, at], targets[i].at[at], out_sems.at[i, at]) for i, at in spots]
+    for copy in ins:
         copy.start()
-    for copy in copies:
+    for arrives, leaves in zip(ins, outs):
+        arrives.wait()
+        leaves.start()
+    for copy in outs:
         copy.wait()
 
 
@@ -510,9 +515,11 @@
     outs = pl.pallas_call(
         hand_over,
         out_shape=[shape] * 4,
-        in_specs=[pl.BlockSpec(memory_space=pltpu.VMEM)] * 4,
+        in_specs=[pl.BlockSpec(memory_space=pl.ANY)] * 4,
         out_specs=[pl.BlockSpec(memory_space=pl.ANY)] * 4,
-        scratch_shapes=[dma((4, 2))],
+        scratch_shapes=[
+            pltpu.VMEM((4, HALF, BLOCK, width), jnp.bfloat16), dma((4, HALF)), dma((4, HALF)),
+        ],
         compiler_params=pltpu.CompilerParams(vmem_limit_bytes=60 * 1024 * 1024),
     )(*outs)
     return tuple(x.reshape(rows, width) for x in outs)

time: 90.7 us -> 86.2 us (0.950)
  the two profiles are of different devices: /device:TPU:0 before, /device:TPU:32 now
where the time goes in v2:
time: 86.2 us; the launch traced here: 86 us
  Pallas kernels  85.4 us (99%)
    pallas_call x1, Pallas kernels, body(): pl.pallas_call(lambda *refs: kernel(frames, *refs), out_shape=[shape] * 4...  82.8 us
    pallas_call x1, Pallas kernels, body(): pl.pallas_call(hand_over, out_shape=[shape] * 4, in_specs=[pl.BlockSpec(m...  2.57 us

profile of v2, /device:TPU:32, one launch (start us, length us, event | category | flops | bytes accessed | tf_op | source)
XLA Modules:
  0.0 86.0 jit_solution(10633710735227637573)
XLA Ops:
  0.6 82.8 %shard_map.93 = (bf16[4,64,1024]{2,1,0:T(8,128)(2,1)}, bf16[4,64,1024]{2,1,0:T(8,128)(2,1)}, bf16[4,64,1024]{2,1,0:T(8,128)(2,1)}, bf16[4,64,1024]{2,1,0:T(8,128)(2,1)}) custom-call(s32[4,13]{1,0:T(4,128)} %refs_0_.1, s32[4]{0:T(128)} %refs_1_.1, bf16[4,64,1024]{2,1,0:T(8,128)(2,1)} %bitcast.8, bf16[4,64,1024]{2,1,0:T(8,128)(2,1)} %bitcast.9, ...), custom_call_target="tpu_custom_call" | custom-call | flops 20937965568 | bytes 4194304 | tf_op jit(solution)/shard_map/pallas_call | solution.py:478
  83.4 2.6 %shard_map.94 = (bf16[4,64,1024]{2,1,0:T(8,128)(2,1)}, bf16[4,64,1024]{2,1,0:T(8,128)(2,1)}, bf16[4,64,1024]{2,1,0:T(8,128)(2,1)}, bf16[4,64,1024]{2,1,0:T(8,128)(2,1)}) custom-call(bf16[4,64,1024]{2,1,0:T(8,128)(2,1)} %get-tuple-element.12.refs_0_, bf16[4,64,1024]{2,1,0:T(8,128)(2,1)} %get-tuple-element.13.refs_1_, ...), custom_call_target="tpu_custom_call" | custom-call | tf_op jit(solution)/shard_map/pallas_call | solution.py:515

commit v3 on v2

--- a/solution.py
+++ b/solution.py
@@ -24,7 +24,7 @@
     frames,
     block_list, block_count, queries, keys, values, out_grad,
     attended, query_grad, key_grad, value_grad,
-    loaded, packed, kv, qd, work, tiles, rows_out, rows_in, give, take, own, final, final_in, relay, meta_vm, meta_sm,
+    loaded, packed, kv, qd, work, low, high, tiles, rows_out, rows_in, give, take, own, final, final_in, relay, meta_vm, meta_sm,
     load_sem, in_send, in_recv, pass_send, pass_recv,
     meta_send, meta_recv, meta_local, row_send, row_recv, row_local,
     term_send, term_recv, grad_send, grad_recv, grad_local, relay_send, relay_recv,
@@ -272,10 +272,32 @@
     spread = jnp.where(
         row_ids == col_ids, jnp.where(col_ids < 2, FACTOR, 1.0), 0.0
     ).astype(jnp.bfloat16)
-    first_head = lax.broadcasted_iota(jnp.int32, (BLOCK, LANES), 1) < HD
-
-    def heads(full):
-        return jnp.where(first_head, full[:HD], full[HD:])
+    apart = jnp.where(row_ids == col_ids, jnp.where(col_ids < 2, FACTOR, 1.0), 0.0)
+    eye = (
+        lax.broadcasted_iota(jnp.int32, (4 * HD, 4 * HD), 0)
+        == lax.broadcasted_iota(jnp.int32, (4 * HD, 4 * HD), 1)
+    ).astype(jnp.bfloat16)
+    gather_rows = (
+        lax.broadcasted_iota(jnp.int32, (BLOCK, 4 * HD), 0)
+        == lax.rem(lax.broadcasted_iota(jnp.int32, (BLOCK, 4 * HD), 1), BLOCK)
+    ).astype(jnp.bfloat16)
+    left_half = lax.broadcasted_iota(jnp.int32, (4 * HD, LANES), 1) < BLOCK
+
+    def across_lanes(left, right):
+        return lax.dot_general(
+            left, right, (((1,), (1,)), ((), ())), preferred_element_type=jnp.float32
+        )
+
+    def turn(step, carry):
+        blocks = [work[4 * step + k] for k in range(4)]
+        straight = across_lanes(eye, jnp.concatenate(blocks, axis=0))
+        crossed = across_lanes(eye, jnp.concatenate([blocks[k ^ 1] for k in range(4)], axis=0))
+        for k in range(4):
+            lanes = slice((k // 2) * LANES, (k // 2 + 1) * LANES)
+            left, right = (straight, crossed) if k % 2 == 0 else (crossed, straight)
+            low[4 * step + k] = jnp.where(left_half, left[:, lanes], 0.0).astype(jnp.bfloat16)
+            high[4 * step + k] = jnp.where(left_half, 0.0, right[:, lanes]).astype(jnp.bfloat16)
+        return carry
 
     def fold(array, op):
         return op(array.reshape(array.shape[0] // 8, 8, LANES), axis=0)
@@ -287,9 +309,7 @@
         picked = jnp.concatenate(
             [work[meta_sm[strip, row, j]] for j in range(SEL)], axis=0
         )
-        both = lax.dot_general(
-            picked, diagonal, (((1,), (1,)), ((), ())), preferred_element_type=jnp.float32
-        )
+        both = across_lanes(picked, diagonal)
         bias = [
             jnp.where(meta_sm[strip, HALF + row, j] > 0, 0.0, MASKED).astype(jnp.float32)
             for j in range(SEL)
@@ -316,12 +336,17 @@
         slab = jnp.concatenate(slabs, axis=0)
         terms = jnp.dot(slab, diagonal, preferred_element_type=jnp.float32)
         tiles[b, :SEL] = terms.reshape(SEL, BLOCK, 2 * LANES)
-        mixed = lax.dot_general(
-            slab, picked, (((0,), (0,)), ((), ())), preferred_element_type=jnp.float32
-        )
-        rows_out[g, b] = jnp.concatenate(
-            [heads(mixed[:LANES, :LANES]) * FACTOR, heads(mixed[LANES:, LANES:])], axis=1
-        ).astype(jnp.bfloat16)
+        turned = []
+        for j in range(0, SEL, 2):
+            pair = low[meta_sm[strip, row, j]]
+            if j + 1 < SEL:
+                pair = pair + high[meta_sm[strip, row, j + 1]]
+            turned.append(pair)
+        padded = jnp.concatenate([slab, jnp.zeros((BLOCK, 2 * LANES), jnp.bfloat16)], axis=0)
+        mixed = jnp.dot(
+            jnp.concatenate(turned, axis=1), padded, preferred_element_type=jnp.float32
+        )
+        rows_out[g, b] = across_lanes(gather_rows, (mixed * apart).astype(jnp.bfloat16)).astype(jnp.bfloat16)
 
     def finish(g):
         slot = lax.rem(g, 2)
@@ -354,6 +379,7 @@
             begin_own(g + 3)
 
         work[...] = kv[g]
+        lax.fori_loop(0, WINDOW // 4, turn, 0)
 
         def four_blocks(i, inner):
             first = lax.rem(HALF * o + HALF * i, FRAME)
@@ -486,6 +512,8 @@
             pltpu.VMEM((GROUPS, WINDOW, BLOCK, 2 * LANES), jnp.bfloat16),
             pltpu.VMEM((GROUPS, FRAME, BLOCK, 2 * LANES), jnp.bfloat16),
             pltpu.VMEM((WINDOW, BLOCK, 2 * LANES), jnp.bfloat16),
+            pltpu.VMEM((WINDOW, 2 * LANES, LANES), jnp.bfloat16),
+            pltpu.VMEM((WINDOW, 2 * LANES, LANES), jnp.bfloat16),
             pltpu.VMEM((FRAME, SEL + 1, BLOCK, 2 * LANES), jnp.float32),
             pltpu.VMEM((GROUPS, FRAME, BLOCK, 2 * LANES), jnp.bfloat16),
             pltpu.VMEM((GROUPS, HALF, BLOCK, 2 * LANES), jnp.bfloat16),

time: 86.2 us -> 90.5 us (1.050)
  Pallas kernels: 85.4 us -> 89.7 us
    pallas_call x1, Pallas kernels: 82.8 us -> 87.1 us  [body(): pl.pallas_call(lambda *refs: kernel(frames, *refs), out_shape=[shape] * 4...]
where the time goes in v3:
time: 90.5 us; the launch traced here: 90.3 us
  Pallas kernels  89.7 us (99%)
    pallas_call x1, Pallas kernels, body(): pl.pallas_call(lambda *refs: kernel(frames, *refs), out_shape=[shape] * 4...  87.1 us
    pallas_call x1, Pallas kernels, body(): pl.pallas_call(hand_over, out_shape=[shape] * 4, in_specs=[pl.BlockSpec(m...  2.57 us

profile of v3, /device:TPU:32, one launch (start us, length us, event | category | flops | bytes accessed | tf_op | source)
XLA Modules:
  0.0 90.3 jit_solution(9312091069941863167)
XLA Ops:
  0.6 87.1 %shard_map.93 = (bf16[4,64,1024]{2,1,0:T(8,128)(2,1)}, bf16[4,64,1024]{2,1,0:T(8,128)(2,1)}, bf16[4,64,1024]{2,1,0:T(8,128)(2,1)}, bf16[4,64,1024]{2,1,0:T(8,128)(2,1)}) custom-call(s32[4,13]{1,0:T(4,128)} %refs_0_.1, s32[4]{0:T(128)} %refs_1_.1, bf16[4,64,1024]{2,1,0:T(8,128)(2,1)} %bitcast.8, bf16[4,64,1024]{2,1,0:T(8,128)(2,1)} %bitcast.9, ...), custom_call_target="tpu_custom_call" | custom-call | flops 20937965568 | bytes 4194304 | tf_op jit(solution)/shard_map/pallas_call | solution.py:504
  87.7 2.6 %shard_map.94 = (bf16[4,64,1024]{2,1,0:T(8,128)(2,1)}, bf16[4,64,1024]{2,1,0:T(8,128)(2,1)}, bf16[4,64,1024]{2,1,0:T(8,128)(2,1)}, bf16[4,64,1024]{2,1,0:T(8,128)(2,1)}) custom-call(bf16[4,64,1024]{2,1,0:T(8,128)(2,1)} %get-tuple-element.12.refs_0_, bf16[4,64,1024]{2,1,0:T(8,128)(2,1)} %get-tuple-element.13.refs_1_, ...), custom_call_target="tpu_custom_call" | custom-call | tf_op jit(solution)/shard_map/pallas_call | solution.py:543

commit v4 on v2

--- a/solution.py
+++ b/solution.py
@@ -282,46 +282,91 @@
 
     def attend(g, b):
         strip, row = b // HALF, lax.rem(b, HALF)
-        part = qd[g, b]
-        diagonal = jnp.concatenate([part] * 4, axis=0) * spread
-        picked = jnp.concatenate(
-            [work[meta_sm[strip, row, j]] for j in range(SEL)], axis=0
-        )
-        both = lax.dot_general(
-            picked, diagonal, (((1,), (1,)), ((), ())), preferred_element_type=jnp.float32
-        )
-        bias = [
-            jnp.where(meta_sm[strip, HALF + row, j] > 0, 0.0, MASKED).astype(jnp.float32)
-            for j in range(SEL)
+        chunks = ((0, 4), (4, 8), (8, SEL))
+        keep = {"slabs": [None] * SEL, "powers": [None] * SEL}
+
+        def diagonal():
+            keep["diagonal"] = jnp.concatenate([qd[g, b]] * 4, axis=0) * spread
+            keep["bias"] = [
+                jnp.where(meta_sm[strip, HALF + row, j] > 0, 0.0, MASKED).astype(jnp.float32)
+                for j in range(SEL)
+            ]
+
+        def products(c):
+            low, high = chunks[c]
+            picked = jnp.concatenate([work[meta_sm[strip, row, j]] for j in range(low, high)], axis=0)
+            keep["picked", c] = picked
+            both = lax.dot_general(
+                picked, keep["diagonal"], (((1,), (1,)), ((), ())), preferred_element_type=jnp.float32
+            )
+            for j in range(low, high):
+                at = slice((j - low) * BLOCK, (j - low + 1) * BLOCK)
+                keep["scores", j] = both[at, :LANES]
+                keep["grad_weights", j] = both[at, LANES:]
+
+        def peak(c):
+            for j in range(*chunks[c]):
+                top = fold(keep["scores", j], jnp.max) + keep["bias"][j]
+                keep["peak"] = jnp.maximum(keep["peak"], top) if j else top
+            if c == len(chunks) - 1:
+                keep["peak"] = jnp.max(keep["peak"], axis=0, keepdims=True)
+
+        def power(j):
+            powers = jnp.exp(keep["scores", j] - (keep["peak"] - keep["bias"][j]))
+            keep["powers"][j] = powers
+            total = fold(powers, jnp.sum)
+            dots = fold(powers * keep["grad_weights", j], jnp.sum)
+            keep["total"] = keep["total"] + total if j else total
+            keep["dots"] = keep["dots"] + dots if j else dots
+            if j == SEL - 1:
+                keep["scale"] = 1.0 / jnp.sum(keep["total"], axis=0, keepdims=True)
+                keep["row_dots"] = jnp.sum(keep["dots"], axis=0, keepdims=True) * keep["scale"]
+
+        def slab(j):
+            weights = keep["powers"][j] * keep["scale"]
+            grad_scores = weights * (keep["grad_weights", j] - keep["row_dots"])
+            keep["slabs"][j] = (grad_scores.astype(jnp.bfloat16), weights.astype(jnp.bfloat16))
+
+        def terms(c):
+            low, high = chunks[c]
+            parts = [jnp.concatenate([pair[k] for pair in keep["slabs"][low:high]], axis=0) for k in range(2)]
+            keep["parts", c] = parts
+            result = jnp.dot(
+                jnp.concatenate(parts, axis=1), keep["diagonal"], preferred_element_type=jnp.float32
+            )
+            tiles[b, low:high] = result.reshape(high - low, BLOCK, 2 * LANES)
+
+        def mixed(c):
+            for k in range(2):
+                lanes = slice(k * LANES, (k + 1) * LANES)
+                product = lax.dot_general(
+                    keep["parts", c][k], keep["picked", c][:, lanes], (((0,), (0,)), ((), ())),
+                    preferred_element_type=jnp.float32,
+                )
+                keep["mixed", k] = keep["mixed", k] + product if c else product
+            if c == len(chunks) - 1:
+                rows_out[g, b] = jnp.concatenate(
+                    [heads(keep["mixed", 0]) * FACTOR, heads(keep["mixed", 1])], axis=1
+                ).astype(jnp.bfloat16)
+
+        def call(function, *args):
+            return lambda: function(*args)
+
+        count = range(len(chunks))
+        return (
+            [diagonal] + [call(products, c) for c in count],
+            [call(peak, c) for c in count] + [call(power, j) for j in range(SEL)] + [call(slab, j) for j in range(SEL)],
+            [call(step, c) for c in count for step in (terms, mixed)],
+        )
+
+    def interleave(stages):
+        placed = [
+            ((k + 0.5) / len(stage), n, step)
+            for n, stage in enumerate(stages)
+            for k, step in enumerate(stage)
         ]
-        parts = [both[j * BLOCK:(j + 1) * BLOCK, :LANES] for j in range(SEL)]
-        peak = fold(parts[0], jnp.max) + bias[0]
-        for j in range(1, SEL):
-            peak = jnp.maximum(peak, fold(parts[j], jnp.max) + bias[j])
-        peak = jnp.max(peak, axis=0, keepdims=True)
-        powers = [jnp.exp(parts[j] - (peak - bias[j])) for j in range(SEL)]
-        grad_weights = [both[j * BLOCK:(j + 1) * BLOCK, LANES:] for j in range(SEL)]
-        total = fold(powers[0], jnp.sum)
-        dots = fold(powers[0] * grad_weights[0], jnp.sum)
-        for j in range(1, SEL):
-            total = total + fold(powers[j], jnp.sum)
-            dots = dots + fold(powers[j] * grad_weights[j], jnp.sum)
-        scale = 1.0 / jnp.sum(total, axis=0, keepdims=True)
-        row_dots = jnp.sum(dots, axis=0, keepdims=True) * scale
-        slabs = []
-        for j in range(SEL):
-            weights = powers[j] * scale
-            grad_scores = weights * (grad_weights[j] - row_dots)
-            slabs.append(jnp.concatenate([grad_scores, weights], axis=1).astype(jnp.bfloat16))
-        slab = jnp.concatenate(slabs, axis=0)
-        terms = jnp.dot(slab, diagonal, preferred_element_type=jnp.float32)
-        tiles[b, :SEL] = terms.reshape(SEL, BLOCK, 2 * LANES)
-        mixed = lax.dot_general(
-            slab, picked, (((0,), (0,)), ((), ())), preferred_element_type=jnp.float32
-        )
-        rows_out[g, b] = jnp.concatenate(
-            [heads(mixed[:LANES, :LANES]) * FACTOR, heads(mixed[LANES:, LANES:])], axis=1
-        ).astype(jnp.bfloat16)
+        for _, _, step in sorted(placed, key=lambda item: item[:2]):
+            step()
 
     def finish(g):
         slot = lax.rem(g, 2)
@@ -355,38 +400,32 @@
 
         work[...] = kv[g]
 
-        def four_blocks(i, inner):
-            first = lax.rem(HALF * o + HALF * i, FRAME)
-            for b in range(HALF):
-                attend(g, first + b)
-
-            @pl.when((i == 0) & (g > 1))
-            def _():
-                finish(g - 2)
-
-            @pl.when(i == 0)
-            def _():
+        blocks = [attend(g, lax.rem(HALF * o + i, FRAME)) for i in range(FRAME)]
+        for turn in range(FRAME + 2):
+            interleave([blocks[turn - k][k] for k in (2, 1, 0) if 0 <= turn - k < FRAME])
+            if turn == HALF + 1:
                 rows_across(g).start()
+
+                @pl.when(g > 1)
+                def _():
+                    finish(g - 2)
 
                 @pl.when(g + 2 < GROUPS)
                 def _():
                     forward(g + 2)
 
-            @pl.when((i == 0) & (g == 0))
-            def _():
-                relay_step(1, 0)
-
-            @pl.when((i == 0) & (g > 0))
-            def _():
-                relay_step(g - 1, 1)
-
-            @pl.when((i == 1) & (g + 2 < GROUPS))
-            def _():
-                relay_step(g + 2, 0)
-
-            return inner
-
-        lax.fori_loop(0, 2, four_blocks, 0)
+                @pl.when(g == 0)
+                def _():
+                    relay_step(1, 0)
+
+                @pl.when(g > 0)
+                def _():
+                    relay_step(g - 1, 1)
+
+        @pl.when(g + 2 < GROUPS)
+        def _():
+            relay_step(g + 2, 0)
+
         for a in range(2):
             rows_along(g, a).start()
 

time: 86.2 us -> 84.1 us (0.976)
  Pallas kernels: 85.4 us -> 83.3 us
    pallas_call x1, Pallas kernels: 82.8 us -> 80.8 us  [body(): pl.pallas_call(lambda *refs: kernel(frames, *refs), out_shape=[shape] * 4...]
where the time goes in v4:
time: 84.1 us; the launch traced here: 84 us
  Pallas kernels  83.3 us (99%)
    pallas_call x1, Pallas kernels, body(): pl.pallas_call(lambda *refs: kernel(frames, *refs), out_shape=[shape] * 4...  80.8 us
    pallas_call x1, Pallas kernels, body(): pl.pallas_call(hand_over, out_shape=[shape] * 4, in_specs=[pl.BlockSpec(m...  2.57 us

profile of v4, /device:TPU:32, one launch (start us, length us, event | category | flops | bytes accessed | tf_op | source)
XLA Modules:
  0.0 84.0 jit_solution(2238613541355641477)
XLA Ops:
  0.6 80.8 %shard_map.93 = (bf16[4,64,1024]{2,1,0:T(8,128)(2,1)}, bf16[4,64,1024]{2,1,0:T(8,128)(2,1)}, bf16[4,64,1024]{2,1,0:T(8,128)(2,1)}, bf16[4,64,1024]{2,1,0:T(8,128)(2,1)}) custom-call(s32[4,13]{1,0:T(4,128)} %refs_0_.1, s32[4]{0:T(128)} %refs_1_.1, bf16[4,64,1024]{2,1,0:T(8,128)(2,1)} %bitcast.8, bf16[4,64,1024]{2,1,0:T(8,128)(2,1)} %bitcast.9, ...), custom_call_target="tpu_custom_call" | custom-call | flops 20937965568 | bytes 4194304 | tf_op jit(solution)/shard_map/pallas_call | solution.py:517
  81.4 2.6 %shard_map.94 = (bf16[4,64,1024]{2,1,0:T(8,128)(2,1)}, bf16[4,64,1024]{2,1,0:T(8,128)(2,1)}, bf16[4,64,1024]{2,1,0:T(8,128)(2,1)}, bf16[4,64,1024]{2,1,0:T(8,128)(2,1)}) custom-call(bf16[4,64,1024]{2,1,0:T(8,128)(2,1)} %get-tuple-element.12.refs_0_, bf16[4,64,1024]{2,1,0:T(8,128)(2,1)} %get-tuple-element.13.refs_1_, ...), custom_call_target="tpu_custom_call" | custom-call | tf_op jit(solution)/shard_map/pallas_call | solution.py:554

commit v5 on v4

--- a/solution.py
+++ b/solution.py
@@ -31,8 +31,7 @@
 ):
     f, s = lax.axis_index("frames"), lax.axis_index("strip")
     o = 1 - s
-    after, before = lax.rem(f + 1, frames), lax.rem(f + frames - 1, frames)
-    partner, next_dev, prev_dev = (f, o), (after, s), (before, s)
+    partner, next_dev, prev_dev = (f, o), (f + 1, s), (f - 1, s)
 
     sources = (keys, values, queries, out_grad)
     loads = [pltpu.make_async_copy(sources[a], loaded.at[a], load_sem.at[a]) for a in range(4)]
@@ -40,23 +39,23 @@
         load.start()
 
     place_in_run = lax.rem(f, RUN)
-    edge = (place_in_run == RUN - 1, place_in_run == 0)
+    has_after, has_before = f < frames - 1, f > 0
+    edge = ((place_in_run == RUN - 1) & has_after, (place_in_run == 0) & has_before)
     part_column = (3 * s, 1 + s)
 
     def relay_of(d, column):
         return (f - 2 * column if d == 0 else f + 2 * column, s)
 
     def relay_to(d, column):
-        if d == 0:
-            return (lax.rem(f + 1 + 2 * column, frames), s)
-        return (lax.rem(f + frames - 1 - 2 * column, frames), s)
+        return (f + 1 + 2 * column if d == 0 else f - 1 - 2 * column, s)
 
     relay_back = 1 - lax.rem(place_in_run, 2)
     relay_column = lax.select(relay_back == 0, (RUN - 1 - place_in_run) // 2, place_in_run // 2)
-    is_relay = ((relay_column == 1) & (s == 0)) | ((relay_column >= 2) & (s == 1))
     relay_half = lax.rem(relay_column, 2)
     relay_source_frame = f - place_in_run + (1 - relay_back) * (RUN - 1)
-    relay_target_frame = lax.rem(relay_source_frame + frames + 1 - 2 * relay_back, frames)
+    relay_target_frame = relay_source_frame + 1 - 2 * relay_back
+    is_relay = ((relay_column == 1) & (s == 0)) | ((relay_column >= 2) & (s == 1))
+    is_relay = is_relay & (relay_target_frame >= 0) & (relay_target_frame < frames)
     relay_target, relay_source = (relay_target_frame, s), (relay_source_frame, s)
 
     barrier = pltpu.get_barrier_semaphore()
@@ -64,8 +63,15 @@
     def greet(device):
         pl.semaphore_signal(barrier, inc=1, device_id=device, device_id_type=MESH)
 
-    for device in (partner, next_dev, prev_dev):
-        greet(device)
+    greet(partner)
+
+    @pl.when(has_after)
+    def _():
+        greet(next_dev)
+
+    @pl.when(has_before)
+    def _():
+        greet(prev_dev)
 
     @pl.when(is_relay)
     def _():
@@ -80,7 +86,8 @@
                 greet(relay_to(d, column))
 
     at_end = (edge[0] | edge[1]).astype(jnp.int32)
-    pl.semaphore_wait(barrier, 3 + 2 * is_relay.astype(jnp.int32) + at_end * (2 + 2 * s))
+    beside = has_after.astype(jnp.int32) + has_before.astype(jnp.int32)
+    pl.semaphore_wait(barrier, 1 + beside + 2 * is_relay.astype(jnp.int32) + at_end * (2 + 2 * s))
 
     def remote(src, dst, send, recv, device):
         return pltpu.make_async_remote_copy(
@@ -113,6 +120,7 @@
             own_rows[:, :, lanes] = loaded[2 * pair + a, :, :, columns(s, g)]
 
     neighbours = (next_dev, prev_dev)
+    sends_to, hears_from = (has_after, has_before), (has_before, has_after)
 
     def start_part(d, part, src, dst, send, recv, phase, g):
         straight = remote(src, dst, send, recv, neighbours[d])
@@ -127,7 +135,7 @@
                 src, relay.at[phase, g], send, relay_recv.at[phase, g], relay_of(d, part_column[part])
             ).start()
 
-        @pl.when(jnp.logical_not(bent))
+        @pl.when(sends_to[d] & jnp.logical_not(bent))
         def _():
             straight.start()
 
@@ -211,14 +219,10 @@
 
     def begin(g):
         for pair in range(2):
-            pack(g, pair)
             swap(g, pair).start()
-
-    def begin_own(g):
-        keep(g, 0)
-        for d in range(2):
-            start_pass(g, d, 0)
-        keep(g, 1)
+            if pair == 0:
+                for d in range(2):
+                    start_pass(g, d, 0)
 
     for pair in range(2):
         loads[2 * pair].wait()
@@ -248,8 +252,6 @@
     meta_vm[s, HALF:] = jnp.zeros((HALF, LANES), jnp.int32)
     meta_vm[s, HALF:, 0:SEL] = usable.astype(jnp.int32)
     share_meta.start()
-    begin(1)
-    begin_own(1)
     tiles[:, SEL] = jnp.zeros((FRAME, BLOCK, 2 * LANES), jnp.float32)
 
     def forward(g):
@@ -257,15 +259,37 @@
         for d in range(2):
             start_pass(g, d, 1)
 
+    def prepare(g, carry):
+        for pair in range(2):
+            pack(g, pair)
+            keep(g, pair)
+        return carry
+
+    lax.fori_loop(1, GROUPS, prepare, 0)
+
+    def clear(w, carry):
+        @pl.when(jnp.logical_not(has_before))
+        def _():
+            for g in range(GROUPS):
+                kv[g, w] = jnp.zeros((BLOCK, 2 * LANES), jnp.bfloat16)
+                take[g, 0, w] = jnp.zeros((BLOCK, 2 * LANES), jnp.bfloat16)
+
+        @pl.when(jnp.logical_not(has_after))
+        def _():
+            for g in range(GROUPS):
+                kv[g, 2 * FRAME + w] = jnp.zeros((BLOCK, 2 * LANES), jnp.bfloat16)
+                take[g, 1, w] = jnp.zeros((BLOCK, 2 * LANES), jnp.bfloat16)
+
+        return carry
+
+    lax.fori_loop(0, FRAME, clear, 0)
     forward(0)
+    begin(1)
     share_meta.wait()
     to_scalar = pltpu.make_async_copy(meta_vm, meta_sm, meta_local)
     to_scalar.start()
     relay_step(0, 0)
-    begin(2)
-    begin_own(2)
     to_scalar.wait()
-    forward(1)
 
     row_ids = lax.broadcasted_iota(jnp.int32, (4 * HD, 4 * HD), 0) // HD
     col_ids = lax.broadcasted_iota(jnp.int32, (4 * HD, 4 * HD), 1) // HD
@@ -371,8 +395,10 @@
     def finish(g):
         slot = lax.rem(g, 2)
         for d in range(2):
-            for part in range(2):
-                wait_terms(g, d, part).wait_recv()
+            @pl.when(hears_from[d])
+            def _():
+                for part in range(2):
+                    wait_terms(g, d, part).wait_recv()
 
         def add(w, carry):
             total = own[slot, w] + take[g, 0, w].astype(jnp.float32) + take[g, 1, w].astype(jnp.float32)
@@ -390,26 +416,33 @@
     def one_group(g, carry):
         swap(g, 1).wait_recv()
         for d in range(2):
-            for part in range(2):
-                wait_pass(g, d, part).wait_recv()
-
-        @pl.when(g + 3 < GROUPS)
-        def _():
-            begin(g + 3)
-            begin_own(g + 3)
+            @pl.when(hears_from[d])
+            def _():
+                for part in range(2):
+                    wait_pass(g, d, part).wait_recv()
+
+        @pl.when(g == 1)
+        def _():
+            begin(3)
 
         work[...] = kv[g]
 
         blocks = [attend(g, lax.rem(HALF * o + i, FRAME)) for i in range(FRAME)]
         for turn in range(FRAME + 2):
             interleave([blocks[turn - k][k] for k in (2, 1, 0) if 0 <= turn - k < FRAME])
+            if turn == 3:
+                @pl.when(g == 0)
+                def _():
+                    forward(1)
+                    begin(2)
+
+                @pl.when(g > 0)
+                def _():
+                    relay_step(g - 1, 1)
+
             if turn == HALF + 1:
                 rows_across(g).start()
-
-                @pl.when(g > 1)
-                def _():
-                    finish(g - 2)
-
+            if turn == 7:
                 @pl.when(g + 2 < GROUPS)
                 def _():
                     forward(g + 2)
@@ -420,7 +453,7 @@
 
                 @pl.when(g > 0)
                 def _():
-                    relay_step(g - 1, 1)
+                    finish(g - 1)
 
         @pl.when(g + 2 < GROUPS)
         def _():
@@ -456,7 +489,6 @@
         return carry
 
     lax.fori_loop(0, GROUPS, one_group, 0)
-    finish(GROUPS - 2)
     relay_step(GROUPS - 1, 1)
     finish(GROUPS - 1)
 
@@ -472,9 +504,11 @@
         for pair in range(2):
             swap(g, pair).wait_send()
         for d in range(2):
-            for part in range(2):
-                wait_pass(g, d, part).wait_send()
-                wait_terms(g, d, part).wait_send()
+            @pl.when(sends_to[d])
+            def _():
+                for part in range(2):
+                    wait_pass(g, d, part).wait_send()
+                    wait_terms(g, d, part).wait_send()
 
         @pl.when(is_relay)
         def _():

time: 84.1 us -> 93.2 us (1.11)
  the two profiles are of different devices: /device:TPU:32 before, /device:TPU:24 now
where the time goes in v5:
time: 93.2 us; the launch traced here: 93.1 us
  Pallas kernels  92.4 us (99%)
    pallas_call x1, Pallas kernels, body(): pl.pallas_call(lambda *refs: kernel(frames, *refs), out_shape=[shape] * 4...  89.9 us
    pallas_call x1, Pallas kernels, body(): pl.pallas_call(hand_over, out_shape=[shape] * 4, in_specs=[pl.BlockSpec(m...  2.57 us

profile of v5, /device:TPU:24, one launch (start us, length us, event | category | flops | bytes accessed | tf_op | source)
XLA Modules:
  0.0 93.1 jit_solution(8165414241843084909)
XLA Ops:
  0.6 89.9 %shard_map.93 = (bf16[4,64,1024]{2,1,0:T(8,128)(2,1)}, bf16[4,64,1024]{2,1,0:T(8,128)(2,1)}, bf16[4,64,1024]{2,1,0:T(8,128)(2,1)}, bf16[4,64,1024]{2,1,0:T(8,128)(2,1)}) custom-call(s32[4,13]{1,0:T(4,128)} %refs_0_.1, s32[4]{0:T(128)} %refs_1_.1, bf16[4,64,1024]{2,1,0:T(8,128)(2,1)} %bitcast.8, bf16[4,64,1024]{2,1,0:T(8,128)(2,1)} %bitcast.9, ...), custom_call_target="tpu_custom_call" | custom-call | flops 20937965568 | bytes 4194304 | tf_op jit(solution)/shard_map/pallas_call | solution.py:551
  90.5 2.6 %shard_map.94 = (bf16[4,64,1024]{2,1,0:T(8,128)(2,1)}, bf16[4,64,1024]{2,1,0:T(8,128)(2,1)}, bf16[4,64,1024]{2,1,0:T(8,128)(2,1)}, bf16[4,64,1024]{2,1,0:T(8,128)(2,1)}) custom-call(bf16[4,64,1024]{2,1,0:T(8,128)(2,1)} %get-tuple-element.12.refs_0_, bf16[4,64,1024]{2,1,0:T(8,128)(2,1)} %get-tuple-element.13.refs_1_, ...), custom_call_target="tpu_custom_call" | custom-call | tf_op jit(solution)/shard_map/pallas_call | solution.py:588

commit v6 on v5

--- a/solution.py
+++ b/solution.py
@@ -223,6 +223,11 @@
             if pair == 0:
                 for d in range(2):
                     start_pass(g, d, 0)
+
+    def pack_keep(g):
+        for pair in range(2):
+            pack(g, pair)
+            keep(g, pair)
 
     for pair in range(2):
         loads[2 * pair].wait()
@@ -252,6 +257,8 @@
     meta_vm[s, HALF:] = jnp.zeros((HALF, LANES), jnp.int32)
     meta_vm[s, HALF:, 0:SEL] = usable.astype(jnp.int32)
     share_meta.start()
+    pack_keep(1)
+    begin(1)
     tiles[:, SEL] = jnp.zeros((FRAME, BLOCK, 2 * LANES), jnp.float32)
 
     def forward(g):
@@ -259,14 +266,6 @@
         for d in range(2):
             start_pass(g, d, 1)
 
-    def prepare(g, carry):
-        for pair in range(2):
-            pack(g, pair)
-            keep(g, pair)
-        return carry
-
-    lax.fori_loop(1, GROUPS, prepare, 0)
-
     def clear(w, carry):
         @pl.when(jnp.logical_not(has_before))
         def _():
@@ -284,12 +283,15 @@
 
     lax.fori_loop(0, FRAME, clear, 0)
     forward(0)
-    begin(1)
+    pack_keep(2)
+    begin(2)
     share_meta.wait()
     to_scalar = pltpu.make_async_copy(meta_vm, meta_sm, meta_local)
     to_scalar.start()
     relay_step(0, 0)
     to_scalar.wait()
+    pack_keep(3)
+    forward(1)
 
     row_ids = lax.broadcasted_iota(jnp.int32, (4 * HD, 4 * HD), 0) // HD
     col_ids = lax.broadcasted_iota(jnp.int32, (4 * HD, 4 * HD), 1) // HD
@@ -421,7 +423,7 @@
                 for part in range(2):
                     wait_pass(g, d, part).wait_recv()
 
-        @pl.when(g == 1)
+        @pl.when(g == 0)
         def _():
             begin(3)
 
@@ -430,30 +432,25 @@
         blocks = [attend(g, lax.rem(HALF * o + i, FRAME)) for i in range(FRAME)]
         for turn in range(FRAME + 2):
             interleave([blocks[turn - k][k] for k in (2, 1, 0) if 0 <= turn - k < FRAME])
-            if turn == 3:
+            if turn == HALF + 1:
+                rows_across(g).start()
+
+                @pl.when(g > 1)
+                def _():
+                    finish(g - 2)
+
+                @pl.when(g + 2 < GROUPS)
+                def _():
+                    forward(g + 2)
+
                 @pl.when(g == 0)
                 def _():
-                    forward(1)
-                    begin(2)
-
+                    relay_step(1, 0)
+
+            if turn == FRAME:
                 @pl.when(g > 0)
                 def _():
                     relay_step(g - 1, 1)
-
-            if turn == HALF + 1:
-                rows_across(g).start()
-            if turn == 7:
-                @pl.when(g + 2 < GROUPS)
-                def _():
-                    forward(g + 2)
-
-                @pl.when(g == 0)
-                def _():
-                    relay_step(1, 0)
-
-                @pl.when(g > 0)
-                def _():
-                    finish(g - 1)
 
         @pl.when(g + 2 < GROUPS)
         def _():
@@ -489,6 +486,7 @@
         return carry
 
     lax.fori_loop(0, GROUPS, one_group, 0)
+    finish(GROUPS - 2)
     relay_step(GROUPS - 1, 1)
     finish(GROUPS - 1)
 

time: 93.2 us -> 81.6 us (0.88)
  the two profiles are of different devices: /device:TPU:24 before, /device:TPU:56 now
where the time goes in v6:
time: 81.6 us; the launch traced here: 81.4 us
  Pallas kernels  80.8 us (99%)
    pallas_call x1, Pallas kernels, body(): pl.pallas_call(lambda *refs: kernel(frames, *refs), out_shape=[shape] * 4...  78.2 us
    pallas_call x1, Pallas kernels, body(): pl.pallas_call(hand_over, out_shape=[shape] * 4, in_specs=[pl.BlockSpec(m...  2.57 us

profile of v6, /device:TPU:56, one launch (start us, length us, event | category | flops | bytes accessed | tf_op | source)
XLA Modules:
  0.0 81.4 jit_solution(454730562247049917)
XLA Ops:
  0.6 78.2 %shard_map.93 = (bf16[4,64,1024]{2,1,0:T(8,128)(2,1)}, bf16[4,64,1024]{2,1,0:T(8,128)(2,1)}, bf16[4,64,1024]{2,1,0:T(8,128)(2,1)}, bf16[4,64,1024]{2,1,0:T(8,128)(2,1)}) custom-call(s32[4,13]{1,0:T(4,128)} %refs_0_.1, s32[4]{0:T(128)} %refs_1_.1, bf16[4,64,1024]{2,1,0:T(8,128)(2,1)} %bitcast.8, bf16[4,64,1024]{2,1,0:T(8,128)(2,1)} %bitcast.9, ...), custom_call_target="tpu_custom_call" | custom-call | flops 20937965568 | bytes 4194304 | tf_op jit(solution)/shard_map/pallas_call | solution.py:549
  78.9 2.6 %shard_map.94 = (bf16[4,64,1024]{2,1,0:T(8,128)(2,1)}, bf16[4,64,1024]{2,1,0:T(8,128)(2,1)}, bf16[4,64,1024]{2,1,0:T(8,128)(2,1)}, bf16[4,64,1024]{2,1,0:T(8,128)(2,1)}) custom-call(bf16[4,64,1024]{2,1,0:T(8,128)(2,1)} %get-tuple-element.12.refs_0_, bf16[4,64,1024]{2,1,0:T(8,128)(2,1)} %get-tuple-element.13.refs_1_, ...), custom_call_target="tpu_custom_call" | custom-call | tf_op jit(solution)/shard_map/pallas_call | solution.py:586

commit v7 on v6

--- a/solution.py
+++ b/solution.py
@@ -217,12 +217,13 @@
 
     share_meta = remote(meta_vm.at[s], meta_vm.at[s], meta_send, meta_recv, partner)
 
-    def begin(g):
-        for pair in range(2):
-            swap(g, pair).start()
-            if pair == 0:
-                for d in range(2):
-                    start_pass(g, d, 0)
+    def begin_keys(g):
+        swap(g, 0).start()
+        for d in range(2):
+            start_pass(g, d, 0)
+
+    def begin_queries(g):
+        swap(g, 1).start()
 
     def pack_keep(g):
         for pair in range(2):
@@ -233,11 +234,11 @@
         loads[2 * pair].wait()
         loads[2 * pair + 1].wait()
         pack(0, pair)
-        swap(0, pair).start()
         keep(0, pair)
         if pair == 0:
-            for d in range(2):
-                start_pass(0, d, 0)
+            begin_keys(0)
+        else:
+            begin_queries(0)
 
     listed = block_list[...]
     row_at = lax.broadcasted_iota(jnp.int32, (HALF, LANES), 0)
@@ -258,7 +259,8 @@
     meta_vm[s, HALF:, 0:SEL] = usable.astype(jnp.int32)
     share_meta.start()
     pack_keep(1)
-    begin(1)
+    begin_keys(1)
+    pack_keep(2)
     tiles[:, SEL] = jnp.zeros((FRAME, BLOCK, 2 * LANES), jnp.float32)
 
     def forward(g):
@@ -283,15 +285,14 @@
 
     lax.fori_loop(0, FRAME, clear, 0)
     forward(0)
-    pack_keep(2)
-    begin(2)
+    begin_keys(2)
+    begin_queries(1)
     share_meta.wait()
     to_scalar = pltpu.make_async_copy(meta_vm, meta_sm, meta_local)
     to_scalar.start()
     relay_step(0, 0)
     to_scalar.wait()
     pack_keep(3)
-    forward(1)
 
     row_ids = lax.broadcasted_iota(jnp.int32, (4 * HD, 4 * HD), 0) // HD
     col_ids = lax.broadcasted_iota(jnp.int32, (4 * HD, 4 * HD), 1) // HD
@@ -423,38 +424,41 @@
                 for part in range(2):
                     wait_pass(g, d, part).wait_recv()
 
-        @pl.when(g == 0)
-        def _():
-            begin(3)
-
         work[...] = kv[g]
 
         blocks = [attend(g, lax.rem(HALF * o + i, FRAME)) for i in range(FRAME)]
         for turn in range(FRAME + 2):
             interleave([blocks[turn - k][k] for k in (2, 1, 0) if 0 <= turn - k < FRAME])
+            if turn == 3:
+                @pl.when(g == 0)
+                def _():
+                    forward(1)
+                    begin_keys(3)
+                    begin_queries(2)
+
+                @pl.when((g > 0) & (g + 1 < GROUPS))
+                def _():
+                    relay_step(g + 1, 0)
+
             if turn == HALF + 1:
                 rows_across(g).start()
+            if turn == 7:
+                @pl.when(g == 0)
+                def _():
+                    begin_queries(3)
+                    relay_step(1, 0)
+
+                @pl.when(g + 2 < GROUPS)
+                def _():
+                    forward(g + 2)
+
+                @pl.when(g > 0)
+                def _():
+                    relay_step(g - 1, 1)
 
                 @pl.when(g > 1)
                 def _():
                     finish(g - 2)
-
-                @pl.when(g + 2 < GROUPS)
-                def _():
-                    forward(g + 2)
-
-                @pl.when(g == 0)
-                def _():
-                    relay_step(1, 0)
-
-            if turn == FRAME:
-                @pl.when(g > 0)
-                def _():
-                    relay_step(g - 1, 1)
-
-        @pl.when(g + 2 < GROUPS)
-        def _():
-            relay_step(g + 2, 0)
 
         for a in range(2):
             rows_along(g, a).start()

time: 81.6 us -> 82 us (level)
  no operation moved by 1% of the time
where the time goes in v7:
time: 82 us; the launch traced here: 81.3 us
  Pallas kernels  80.7 us (98%)
    pallas_call x1, Pallas kernels, body(): pl.pallas_call(lambda *refs: kernel(frames, *refs), out_shape=[shape] * 4...  78.1 us
    pallas_call x1, Pallas kernels, body(): pl.pallas_call(hand_over, out_shape=[shape] * 4, in_specs=[pl.BlockSpec(m...  2.57 us

profile of v7, /device:TPU:56, one launch (start us, length us, event | category | flops | bytes accessed | tf_op | source)
XLA Modules:
  0.0 81.3 jit_solution(14047262421746241725)
XLA Ops:
  0.6 78.1 %shard_map.93 = (bf16[4,64,1024]{2,1,0:T(8,128)(2,1)}, bf16[4,64,1024]{2,1,0:T(8,128)(2,1)}, bf16[4,64,1024]{2,1,0:T(8,128)(2,1)}, bf16[4,64,1024]{2,1,0:T(8,128)(2,1)}) custom-call(s32[4,13]{1,0:T(4,128)} %refs_0_.1, s32[4]{0:T(128)} %refs_1_.1, bf16[4,64,1024]{2,1,0:T(8,128)(2,1)} %bitcast.8, bf16[4,64,1024]{2,1,0:T(8,128)(2,1)} %bitcast.9, ...), custom_call_target="tpu_custom_call" | custom-call | flops 20937965568 | bytes 4194304 | tf_op jit(solution)/shard_map/pallas_call | solution.py:553
  78.8 2.6 %shard_map.94 = (bf16[4,64,1024]{2,1,0:T(8,128)(2,1)}, bf16[4,64,1024]{2,1,0:T(8,128)(2,1)}, bf16[4,64,1024]{2,1,0:T(8,128)(2,1)}, bf16[4,64,1024]{2,1,0:T(8,128)(2,1)}) custom-call(bf16[4,64,1024]{2,1,0:T(8,128)(2,1)} %get-tuple-element.12.refs_0_, bf16[4,64,1024]{2,1,0:T(8,128)(2,1)} %get-tuple-element.13.refs_1_, ...), custom_call_target="tpu_custom_call" | custom-call | tf_op jit(solution)/shard_map/pallas_call | solution.py:590

commit v8 on v7

--- a/solution.py
+++ b/solution.py
@@ -440,8 +440,10 @@
                 def _():
                     relay_step(g + 1, 0)
 
-            if turn == HALF + 1:
-                rows_across(g).start()
+                @pl.when(g == GROUPS - 1)
+                def _():
+                    rows_across(GROUPS - 2).start()
+
             if turn == 7:
                 @pl.when(g == 0)
                 def _():
@@ -455,6 +457,10 @@
                 @pl.when(g > 0)
                 def _():
                     relay_step(g - 1, 1)
+
+                @pl.when((g > 0) & (g < GROUPS - 1))
+                def _():
+                    rows_across(g - 1).start()
 
                 @pl.when(g > 1)
                 def _():
@@ -490,8 +496,9 @@
         return carry
 
     lax.fori_loop(0, GROUPS, one_group, 0)
+    relay_step(GROUPS - 1, 1)
+    rows_across(GROUPS - 1).start()
     finish(GROUPS - 2)
-    relay_step(GROUPS - 1, 1)
     finish(GROUPS - 1)
 
     def land(g, carry):

time: 82 us -> 78.9 us (0.962)
  Pallas kernels: 80.7 us -> 78.1 us
    pallas_call x1, Pallas kernels: 78.1 us -> 75.5 us  [body(): pl.pallas_call(lambda *refs: kernel(frames, *refs), out_shape=[shape] * 4...]
where the time goes in v8:
time: 78.9 us; the launch traced here: 78.8 us
  Pallas kernels  78.1 us (99%)
    pallas_call x1, Pallas kernels, body(): pl.pallas_call(lambda *refs: kernel(frames, *refs), out_shape=[shape] * 4...  75.5 us
    pallas_call x1, Pallas kernels, body(): pl.pallas_call(hand_over, out_shape=[shape] * 4, in_specs=[pl.BlockSpec(m...  2.57 us

profile of v8, /device:TPU:56, one launch (start us, length us, event | category | flops | bytes accessed | tf_op | source)
XLA Modules:
  0.0 78.8 jit_solution(11312839637601127867)
XLA Ops:
  0.6 75.5 %shard_map.93 = (bf16[4,64,1024]{2,1,0:T(8,128)(2,1)}, bf16[4,64,1024]{2,1,0:T(8,128)(2,1)}, bf16[4,64,1024]{2,1,0:T(8,128)(2,1)}, bf16[4,64,1024]{2,1,0:T(8,128)(2,1)}) custom-call(s32[4,13]{1,0:T(4,128)} %refs_0_.1, s32[4]{0:T(128)} %refs_1_.1, bf16[4,64,1024]{2,1,0:T(8,128)(2,1)} %bitcast.8, bf16[4,64,1024]{2,1,0:T(8,128)(2,1)} %bitcast.9, ...), custom_call_target="tpu_custom_call" | custom-call | flops 20937965568 | bytes 4194304 | tf_op jit(solution)/shard_map/pallas_call | solution.py:560
  76.2 2.6 %shard_map.94 = (bf16[4,64,1024]{2,1,0:T(8,128)(2,1)}, bf16[4,64,1024]{2,1,0:T(8,128)(2,1)}, bf16[4,64,1024]{2,1,0:T(8,128)(2,1)}, bf16[4,64,1024]{2,1,0:T(8,128)(2,1)}) custom-call(bf16[4,64,1024]{2,1,0:T(8,128)(2,1)} %get-tuple-element.12.refs_0_, bf16[4,64,1024]{2,1,0:T(8,128)(2,1)} %get-tuple-element.13.refs_1_, ...), custom_call_target="tpu_custom_call" | custom-call | tf_op jit(solution)/shard_map/pallas_call | solution.py:597

commit v9 on v8

--- a/solution.py
+++ b/solution.py
@@ -440,9 +440,13 @@
                 def _():
                     relay_step(g + 1, 0)
 
-                @pl.when(g == GROUPS - 1)
+                @pl.when(g == 1)
                 def _():
-                    rows_across(GROUPS - 2).start()
+                    rows_across(0).start()
+
+                @pl.when(g > 1)
+                def _():
+                    finish(g - 2)
 
             if turn == 7:
                 @pl.when(g == 0)
@@ -457,14 +461,6 @@
                 @pl.when(g > 0)
                 def _():
                     relay_step(g - 1, 1)
-
-                @pl.when((g > 0) & (g < GROUPS - 1))
-                def _():
-                    rows_across(g - 1).start()
-
-                @pl.when(g > 1)
-                def _():
-                    finish(g - 2)
 
         for a in range(2):
             rows_along(g, a).start()
@@ -486,6 +482,10 @@
         for d in range(2):
             for part in range(2):
                 start_terms(g, d, part)
+
+        @pl.when((g > 0) & (g < GROUPS - 1))
+        def _():
+            rows_across(g).start()
 
         def collect_own(w, inner):
             own[lax.rem(g, 2), w] = gather(w, FRAME)

time: 78.9 us -> 79.4 us (level)
  no operation moved by 1% of the time
where the time goes in v9:
time: 79.4 us; the launch traced here: 79.1 us
  Pallas kernels  78.4 us (99%)
    pallas_call x1, Pallas kernels, body(): pl.pallas_call(lambda *refs: kernel(frames, *refs), out_shape=[shape] * 4...  75.9 us
    pallas_call x1, Pallas kernels, body(): pl.pallas_call(hand_over, out_shape=[shape] * 4, in_specs=[pl.BlockSpec(m...  2.57 us

profile of v9, /device:TPU:56, one launch (start us, length us, event | category | flops | bytes accessed | tf_op | source)
XLA Modules:
  0.0 79.1 jit_solution(15092626041485944389)
XLA Ops:
  0.6 75.9 %shard_map.93 = (bf16[4,64,1024]{2,1,0:T(8,128)(2,1)}, bf16[4,64,1024]{2,1,0:T(8,128)(2,1)}, bf16[4,64,1024]{2,1,0:T(8,128)(2,1)}, bf16[4,64,1024]{2,1,0:T(8,128)(2,1)}) custom-call(s32[4,13]{1,0:T(4,128)} %refs_0_.1, s32[4]{0:T(128)} %refs_1_.1, bf16[4,64,1024]{2,1,0:T(8,128)(2,1)} %bitcast.8, bf16[4,64,1024]{2,1,0:T(8,128)(2,1)} %bitcast.9, ...), custom_call_target="tpu_custom_call" | custom-call | flops 20937965568 | bytes 4194304 | tf_op jit(solution)/shard_map/pallas_call | solution.py:560
  76.5 2.6 %shard_map.94 = (bf16[4,64,1024]{2,1,0:T(8,128)(2,1)}, bf16[4,64,1024]{2,1,0:T(8,128)(2,1)}, bf16[4,64,1024]{2,1,0:T(8,128)(2,1)}, bf16[4,64,1024]{2,1,0:T(8,128)(2,1)}) custom-call(bf16[4,64,1024]{2,1,0:T(8,128)(2,1)} %get-tuple-element.12.refs_0_, bf16[4,64,1024]{2,1,0:T(8,128)(2,1)} %get-tuple-element.13.refs_1_, ...), custom_call_target="tpu_custom_call" | custom-call | tf_op jit(solution)/shard_map/pallas_call | solution.py:597

commit v10 on v8

--- a/solution.py
+++ b/solution.py
@@ -27,7 +27,7 @@
     loaded, packed, kv, qd, work, tiles, rows_out, rows_in, give, take, own, final, final_in, relay, meta_vm, meta_sm,
     load_sem, in_send, in_recv, pass_send, pass_recv,
     meta_send, meta_recv, meta_local, row_send, row_recv, row_local,
-    term_send, term_recv, grad_send, grad_recv, grad_local, relay_send, relay_recv,
+    term_send, term_recv, grad_send, grad_recv, grad_local, relay_send, relay_recv, slant_send,
 ):
     f, s = lax.axis_index("frames"), lax.axis_index("strip")
     o = 1 - s
@@ -85,9 +85,17 @@
                 greet(relay_of(d, column))
                 greet(relay_to(d, column))
 
+    slant = (edge[0] & (s == 1), edge[1] & (s == 0))
+    slant_to = ((f + 1, 0), (f - 1, 1))
+    for d in range(2):
+        @pl.when(slant[d])
+        def _():
+            greet(slant_to[d])
+
     at_end = (edge[0] | edge[1]).astype(jnp.int32)
+    slants = (slant[0] | slant[1]).astype(jnp.int32)
     beside = has_after.astype(jnp.int32) + has_before.astype(jnp.int32)
-    pl.semaphore_wait(barrier, 1 + beside + 2 * is_relay.astype(jnp.int32) + at_end * (2 + 2 * s))
+    pl.semaphore_wait(barrier, 1 + beside + slants + 2 * is_relay.astype(jnp.int32) + at_end * (2 + 2 * s))
 
     def remote(src, dst, send, recv, device):
         return pltpu.make_async_remote_copy(
@@ -122,10 +130,17 @@
     neighbours = (next_dev, prev_dev)
     sends_to, hears_from = (has_after, has_before), (has_before, has_after)
 
+    def skipped(d, g):
+        return edge[d] & (s == d) & (g == 0)
+
     def start_part(d, part, src, dst, send, recv, phase, g):
         straight = remote(src, dst, send, recv, neighbours[d])
+        starts = sends_to[d]
         if part == 0:
             bent = edge[d] & (s == 1)
+        elif phase == 0:
+            bent = edge[d] & (g > 0)
+            starts = starts & jnp.logical_not(skipped(d, g))
         else:
             bent = edge[d]
 
@@ -135,7 +150,7 @@
                 src, relay.at[phase, g], send, relay_recv.at[phase, g], relay_of(d, part_column[part])
             ).start()
 
-        @pl.when(sends_to[d] & jnp.logical_not(bent))
+        @pl.when(starts & jnp.logical_not(bent))
         def _():
             straight.start()
 
@@ -177,8 +192,17 @@
             recv = term_recv.at[g, relay_back, relay_half]
         return remote(relay.at[phase, g], target, relay_send.at[phase, g], recv, relay_target)
 
+    def relays(g, phase):
+        return is_relay & ((relay_column == 3) | (g > 0)) if phase == 0 else is_relay
+
+    def slant_copy(d):
+        base = (0, 2 * FRAME)[d]
+        return remote(
+            packed.at[0, 0], kv_window(0, base, s), slant_send, pass_recv.at[0, d, s], slant_to[d]
+        )
+
     def relay_step(g, phase):
-        @pl.when(is_relay)
+        @pl.when(relays(g, phase))
         def _():
             remote(
                 relay.at[phase, g], relay.at[phase, g], relay_send.at[phase, g],
@@ -237,6 +261,10 @@
         keep(0, pair)
         if pair == 0:
             begin_keys(0)
+            for d in range(2):
+                @pl.when(slant[d])
+                def _():
+                    slant_copy(d).start()
         else:
             begin_queries(0)
 
@@ -284,13 +312,13 @@
         return carry
 
     lax.fori_loop(0, FRAME, clear, 0)
+    relay_step(0, 0)
     forward(0)
     begin_keys(2)
     begin_queries(1)
     share_meta.wait()
     to_scalar = pltpu.make_async_copy(meta_vm, meta_sm, meta_local)
     to_scalar.start()
-    relay_step(0, 0)
     to_scalar.wait()
     pack_keep(3)
 
@@ -516,12 +544,16 @@
             @pl.when(sends_to[d])
             def _():
                 for part in range(2):
-                    wait_pass(g, d, part).wait_send()
                     wait_terms(g, d, part).wait_send()
-
-        @pl.when(is_relay)
-        def _():
-            for phase in range(2):
+                wait_pass(g, d, 0).wait_send()
+
+                @pl.when(jnp.logical_not(skipped(d, g)))
+                def _():
+                    wait_pass(g, d, 1).wait_send()
+
+        for phase in range(2):
+            @pl.when(relays(g, phase))
+            def _():
                 relay_on(g, phase).wait_send()
 
         rows_across(g).wait_send()
@@ -534,6 +566,10 @@
         return carry
 
     lax.fori_loop(0, GROUPS, drain, 0)
+    for d in range(2):
+        @pl.when(slant[d])
+        def _():
+            slant_copy(d).wait_send()
 
 
 def hand_over(*refs):
@@ -585,7 +621,7 @@
             dma((GROUPS,)), dma((GROUPS,)), dma((2 * GROUPS, 2)),
             dma((GROUPS, 2, 2)), dma((GROUPS, 2, 2)),
             dma((GROUPS,)), dma((GROUPS,)), dma((2 * GROUPS, 2)),
-            dma((2, GROUPS)), dma((2, GROUPS)),
+            dma((2, GROUPS)), dma((2, GROUPS)), dma,
         ],
         cost_estimate=pl.CostEstimate(
             flops=flops, bytes_accessed=16 * rows * width, transcendentals=FRAME * SEL * BLOCK * LANES * GROUPS

time: 78.9 us -> 76.2 us (0.966)
  Pallas kernels: 78.1 us -> 75.4 us
    pallas_call x1, Pallas kernels: 75.5 us -> 72.8 us  [body(): pl.pallas_call(lambda *refs: kernel(frames, *refs), out_shape=[shape] * 4...]
where the time goes in v10:
time: 76.2 us; the launch traced here: 76 us
  Pallas kernels  75.4 us (99%)
    pallas_call x1, Pallas kernels, body(): pl.pallas_call(lambda *refs: kernel(frames, *refs), out_shape=[shape] * 4...  72.8 us
    pallas_call x1, Pallas kernels, body(): pl.pallas_call(hand_over, out_shape=[shape] * 4, in_specs=[pl.BlockSpec(m...  2.57 us

profile of v10, /device:TPU:56, one launch (start us, length us, event | category | flops | bytes accessed | tf_op | source)
XLA Modules:
  0.0 76.0 jit_solution(6746648434852486601)
XLA Ops:
  0.6 72.8 %shard_map.93 = (bf16[4,64,1024]{2,1,0:T(8,128)(2,1)}, bf16[4,64,1024]{2,1,0:T(8,128)(2,1)}, bf16[4,64,1024]{2,1,0:T(8,128)(2,1)}, bf16[4,64,1024]{2,1,0:T(8,128)(2,1)}) custom-call(s32[4,13]{1,0:T(4,128)} %refs_0_.1, s32[4]{0:T(128)} %refs_1_.1, bf16[4,64,1024]{2,1,0:T(8,128)(2,1)} %bitcast.8, bf16[4,64,1024]{2,1,0:T(8,128)(2,1)} %bitcast.9, ...), custom_call_target="tpu_custom_call" | custom-call | flops 20937965568 | bytes 4194304 | tf_op jit(solution)/shard_map/pallas_call | solution.py:596
  73.5 2.6 %shard_map.94 = (bf16[4,64,1024]{2,1,0:T(8,128)(2,1)}, bf16[4,64,1024]{2,1,0:T(8,128)(2,1)}, bf16[4,64,1024]{2,1,0:T(8,128)(2,1)}, bf16[4,64,1024]{2,1,0:T(8,128)(2,1)}) custom-call(bf16[4,64,1024]{2,1,0:T(8,128)(2,1)} %get-tuple-element.12.refs_0_, bf16[4,64,1024]{2,1,0:T(8,128)(2,1)} %get-tuple-element.13.refs_1_, ...), custom_call_target="tpu_custom_call" | custom-call | tf_op jit(solution)/shard_map/pallas_call | solution.py:633

commit v11 on v10

--- a/solution.py
+++ b/solution.py
@@ -436,8 +436,9 @@
             final[g, w] = total.astype(jnp.bfloat16)
             return carry
 
-        lax.fori_loop(0, FRAME, add, 0)
+        lax.fori_loop(HALF * o, HALF * o + HALF, add, 0)
         grads_across(g).start()
+        lax.fori_loop(HALF * s, HALF * s + HALF, add, 0)
         for a in range(2):
             grads_along(g, a).start()
         rows_across(g).wait_recv()
@@ -471,6 +472,7 @@
                 @pl.when(g == GROUPS - 1)
                 def _():
                     rows_across(GROUPS - 2).start()
+                    finish(GROUPS - 3)
 
             if turn == 7:
                 @pl.when(g == 0)
@@ -490,7 +492,11 @@
                 def _():
                     rows_across(g - 1).start()
 
-                @pl.when(g > 1)
+                @pl.when(g == GROUPS - 1)
+                def _():
+                    rows_across(g).start()
+
+                @pl.when(g == GROUPS - 2)
                 def _():
                     finish(g - 2)
 
@@ -510,9 +516,9 @@
             give[g, 0, w] = gather(w, 2 * FRAME).astype(jnp.bfloat16)
             return inner
 
-        lax.fori_loop(0, FRAME, collect, 0)
-        for d in range(2):
-            for part in range(2):
+        for part, half in ((1, o), (0, s)):
+            lax.fori_loop(HALF * half, HALF * half + HALF, collect, 0)
+            for d in range(2):
                 start_terms(g, d, part)
 
         def collect_own(w, inner):
@@ -524,9 +530,8 @@
         return carry
 
     lax.fori_loop(0, GROUPS, one_group, 0)
+    finish(GROUPS - 2)
     relay_step(GROUPS - 1, 1)
-    rows_across(GROUPS - 1).start()
-    finish(GROUPS - 2)
     finish(GROUPS - 1)
 
     def land(g, carry):

time: 76.2 us -> 78.7 us (1.033)
  Pallas kernels: 75.4 us -> 77.9 us
    pallas_call x1, Pallas kernels: 72.8 us -> 75.3 us  [body(): pl.pallas_call(lambda *refs: kernel(frames, *refs), out_shape=[shape] * 4...]
where the time goes in v11:
time: 78.7 us; the launch traced here: 78.5 us
  Pallas kernels  77.9 us (99%)
    pallas_call x1, Pallas kernels, body(): pl.pallas_call(lambda *refs: kernel(frames, *refs), out_shape=[shape] * 4...  75.3 us
    pallas_call x1, Pallas kernels, body(): pl.pallas_call(hand_over, out_shape=[shape] * 4, in_specs=[pl.BlockSpec(m...  2.57 us

profile of v11, /device:TPU:56, one launch (start us, length us, event | category | flops | bytes accessed | tf_op | source)
XLA Modules:
  0.0 78.5 jit_solution(2664732763543148367)
XLA Ops:
  0.6 75.3 %shard_map.93 = (bf16[4,64,1024]{2,1,0:T(8,128)(2,1)}, bf16[4,64,1024]{2,1,0:T(8,128)(2,1)}, bf16[4,64,1024]{2,1,0:T(8,128)(2,1)}, bf16[4,64,1024]{2,1,0:T(8,128)(2,1)}) custom-call(s32[4,13]{1,0:T(4,128)} %refs_0_.1, s32[4]{0:T(128)} %refs_1_.1, bf16[4,64,1024]{2,1,0:T(8,128)(2,1)} %bitcast.8, bf16[4,64,1024]{2,1,0:T(8,128)(2,1)} %bitcast.9, ...), custom_call_target="tpu_custom_call" | custom-call | flops 20937965568 | bytes 4194304 | tf_op jit(solution)/shard_map/pallas_call | solution.py:601
  75.9 2.6 %shard_map.94 = (bf16[4,64,1024]{2,1,0:T(8,128)(2,1)}, bf16[4,64,1024]{2,1,0:T(8,128)(2,1)}, bf16[4,64,1024]{2,1,0:T(8,128)(2,1)}, bf16[4,64,1024]{2,1,0:T(8,128)(2,1)}) custom-call(bf16[4,64,1024]{2,1,0:T(8,128)(2,1)} %get-tuple-element.12.refs_0_, bf16[4,64,1024]{2,1,0:T(8,128)(2,1)} %get-tuple-element.13.refs_1_, ...), custom_call_target="tpu_custom_call" | custom-call | tf_op jit(solution)/shard_map/pallas_call | solution.py:638

commit v12 on v10

--- a/solution.py
+++ b/solution.py
@@ -287,7 +287,6 @@
     meta_vm[s, HALF:, 0:SEL] = usable.astype(jnp.int32)
     share_meta.start()
     pack_keep(1)
-    begin_keys(1)
     pack_keep(2)
     tiles[:, SEL] = jnp.zeros((FRAME, BLOCK, 2 * LANES), jnp.float32)
 
@@ -314,8 +313,7 @@
     lax.fori_loop(0, FRAME, clear, 0)
     relay_step(0, 0)
     forward(0)
-    begin_keys(2)
-    begin_queries(1)
+    begin_keys(1)
     share_meta.wait()
     to_scalar = pltpu.make_async_copy(meta_vm, meta_sm, meta_local)
     to_scalar.start()
@@ -452,6 +450,11 @@
                 for part in range(2):
                     wait_pass(g, d, part).wait_recv()
 
+        @pl.when(g == 0)
+        def _():
+            begin_keys(2)
+            begin_queries(1)
+
         work[...] = kv[g]
 
         blocks = [attend(g, lax.rem(HALF * o + i, FRAME)) for i in range(FRAME)]
@@ -510,9 +513,9 @@
             give[g, 0, w] = gather(w, 2 * FRAME).astype(jnp.bfloat16)
             return inner
 
-        lax.fori_loop(0, FRAME, collect, 0)
-        for d in range(2):
-            for part in range(2):
+        for part, half in ((1, o), (0, s)):
+            lax.fori_loop(HALF * half, HALF * half + HALF, collect, 0)
+            for d in range(2):
                 start_terms(g, d, part)
 
         def collect_own(w, inner):
@@ -526,8 +529,16 @@
     lax.fori_loop(0, GROUPS, one_group, 0)
     relay_step(GROUPS - 1, 1)
     rows_across(GROUPS - 1).start()
-    finish(GROUPS - 2)
+
+    @pl.when(at_end > 0)
+    def _():
+        finish(GROUPS - 2)
+
     finish(GROUPS - 1)
+
+    @pl.when(at_end == 0)
+    def _():
+        finish(GROUPS - 2)
 
     def land(g, carry):
         grads_across(g).wait_recv()

time: 76.2 us -> 77 us (1.010)
  Pallas kernels: 75.4 us -> 76.2 us
where the time goes in v12:
time: 77 us; the launch traced here: 76.8 us
  Pallas kernels  76.2 us (99%)
    pallas_call x1, Pallas kernels, body(): pl.pallas_call(lambda *refs: kernel(frames, *refs), out_shape=[shape] * 4...  73.6 us
    pallas_call x1, Pallas kernels, body(): pl.pallas_call(hand_over, out_shape=[shape] * 4, in_specs=[pl.BlockSpec(m...  2.57 us

profile of v12, /device:TPU:56, one launch (start us, length us, event | category | flops | bytes accessed | tf_op | source)
XLA Modules:
  0.0 76.8 jit_solution(5404256064160658341)
XLA Ops:
  0.6 73.6 %shard_map.93 = (bf16[4,64,1024]{2,1,0:T(8,128)(2,1)}, bf16[4,64,1024]{2,1,0:T(8,128)(2,1)}, bf16[4,64,1024]{2,1,0:T(8,128)(2,1)}, bf16[4,64,1024]{2,1,0:T(8,128)(2,1)}) custom-call(s32[4,13]{1,0:T(4,128)} %refs_0_.1, s32[4]{0:T(128)} %refs_1_.1, bf16[4,64,1024]{2,1,0:T(8,128)(2,1)} %bitcast.8, bf16[4,64,1024]{2,1,0:T(8,128)(2,1)} %bitcast.9, ...), custom_call_target="tpu_custom_call" | custom-call | flops 20937965568 | bytes 4194304 | tf_op jit(solution)/shard_map/pallas_call | solution.py:607
  74.2 2.6 %shard_map.94 = (bf16[4,64,1024]{2,1,0:T(8,128)(2,1)}, bf16[4,64,1024]{2,1,0:T(8,128)(2,1)}, bf16[4,64,1024]{2,1,0:T(8,128)(2,1)}, bf16[4,64,1024]{2,1,0:T(8,128)(2,1)}) custom-call(bf16[4,64,1024]{2,1,0:T(8,128)(2,1)} %get-tuple-element.12.refs_0_, bf16[4,64,1024]{2,1,0:T(8,128)(2,1)} %get-tuple-element.13.refs_1_, ...), custom_call_target="tpu_custom_call" | custom-call | tf_op jit(solution)/shard_map/pallas_call | solution.py:644

commit v13 on v10

--- a/solution.py
+++ b/solution.py
@@ -130,8 +130,7 @@
     neighbours = (next_dev, prev_dev)
     sends_to, hears_from = (has_after, has_before), (has_before, has_after)
 
-    def skipped(d, g):
-        return edge[d] & (s == d) & (g == 0)
+    skipped = (edge[0] & (s == 0), edge[1] & (s == 1))
 
     def start_part(d, part, src, dst, send, recv, phase, g):
         straight = remote(src, dst, send, recv, neighbours[d])
@@ -139,8 +138,8 @@
         if part == 0:
             bent = edge[d] & (s == 1)
         elif phase == 0:
-            bent = edge[d] & (g > 0)
-            starts = starts & jnp.logical_not(skipped(d, g))
+            bent = edge[d] & (s != d) & (g > 0)
+            starts = starts & jnp.logical_not(skipped[d])
         else:
             bent = edge[d]
 
@@ -193,12 +192,14 @@
         return remote(relay.at[phase, g], target, relay_send.at[phase, g], recv, relay_target)
 
     def relays(g, phase):
-        return is_relay & ((relay_column == 3) | (g > 0)) if phase == 0 else is_relay
-
-    def slant_copy(d):
+        if phase == 0:
+            return is_relay & ((relay_column == 3) | ((relay_column == 2 - relay_back) & (g > 0)))
+        return is_relay
+
+    def slant_copy(g, d):
         base = (0, 2 * FRAME)[d]
         return remote(
-            packed.at[0, 0], kv_window(0, base, s), slant_send, pass_recv.at[0, d, s], slant_to[d]
+            packed.at[g, 0], kv_window(g, base, s), slant_send.at[g], pass_recv.at[g, d, s], slant_to[d]
         )
 
     def relay_step(g, phase):
@@ -246,6 +247,10 @@
         for d in range(2):
             start_pass(g, d, 0)
 
+            @pl.when(slant[d])
+            def _():
+                slant_copy(g, d).start()
+
     def begin_queries(g):
         swap(g, 1).start()
 
@@ -261,10 +266,6 @@
         keep(0, pair)
         if pair == 0:
             begin_keys(0)
-            for d in range(2):
-                @pl.when(slant[d])
-                def _():
-                    slant_copy(d).start()
         else:
             begin_queries(0)
 
@@ -547,9 +548,13 @@
                     wait_terms(g, d, part).wait_send()
                 wait_pass(g, d, 0).wait_send()
 
-                @pl.when(jnp.logical_not(skipped(d, g)))
+                @pl.when(jnp.logical_not(skipped[d]))
                 def _():
                     wait_pass(g, d, 1).wait_send()
+
+                @pl.when(slant[d])
+                def _():
+                    slant_copy(g, d).wait_send()
 
         for phase in range(2):
             @pl.when(relays(g, phase))
@@ -566,10 +571,6 @@
         return carry
 
     lax.fori_loop(0, GROUPS, drain, 0)
-    for d in range(2):
-        @pl.when(slant[d])
-        def _():
-            slant_copy(d).wait_send()
 
 
 def hand_over(*refs):
@@ -621,7 +622,7 @@
             dma((GROUPS,)), dma((GROUPS,)), dma((2 * GROUPS, 2)),
             dma((GROUPS, 2, 2)), dma((GROUPS, 2, 2)),
             dma((GROUPS,)), dma((GROUPS,)), dma((2 * GROUPS, 2)),
-            dma((2, GROUPS)), dma((2, GROUPS)), dma,
+            dma((2, GROUPS)), dma((2, GROUPS)), dma((GROUPS,)),
         ],
         cost_estimate=pl.CostEstimate(
             flops=flops, bytes_accessed=16 * rows * width, transcendentals=FRAME * SEL * BLOCK * LANES * GROUPS

time: 76.2 us -> 74.5 us (0.978)
  Pallas kernels: 75.4 us -> 73.3 us
    pallas_call x1, Pallas kernels: 72.8 us -> 70.7 us  [body(): pl.pallas_call(lambda *refs: kernel(frames, *refs), out_shape=[shape] * 4...]
where the time goes in v13:
time: 74.5 us; the launch traced here: 74 us
  Pallas kernels  73.3 us (98%)
    pallas_call x1, Pallas kernels, body(): pl.pallas_call(lambda *refs: kernel(frames, *refs), out_shape=[shape] * 4...  70.7 us
    pallas_call x1, Pallas kernels, body(): pl.pallas_call(hand_over, out_shape=[shape] * 4, in_specs=[pl.BlockSpec(m...  2.57 us

profile of v13, /device:TPU:56, one launch (start us, length us, event | category | flops | bytes accessed | tf_op | source)
XLA Modules:
  0.0 74.0 jit_solution(11216480584359206898)
XLA Ops:
  0.6 70.7 %shard_map.93 = (bf16[4,64,1024]{2,1,0:T(8,128)(2,1)}, bf16[4,64,1024]{2,1,0:T(8,128)(2,1)}, bf16[4,64,1024]{2,1,0:T(8,128)(2,1)}, bf16[4,64,1024]{2,1,0:T(8,128)(2,1)}) custom-call(s32[4,13]{1,0:T(4,128)} %refs_0_.1, s32[4]{0:T(128)} %refs_1_.1, bf16[4,64,1024]{2,1,0:T(8,128)(2,1)} %bitcast.8, bf16[4,64,1024]{2,1,0:T(8,128)(2,1)} %bitcast.9, ...), custom_call_target="tpu_custom_call" | custom-call | flops 20937965568 | bytes 4194304 | tf_op jit(solution)/shard_map/pallas_call | solution.py:597
  71.4 2.6 %shard_map.94 = (bf16[4,64,1024]{2,1,0:T(8,128)(2,1)}, bf16[4,64,1024]{2,1,0:T(8,128)(2,1)}, bf16[4,64,1024]{2,1,0:T(8,128)(2,1)}, bf16[4,64,1024]{2,1,0:T(8,128)(2,1)}) custom-call(bf16[4,64,1024]{2,1,0:T(8,128)(2,1)} %get-tuple-element.12.refs_0_, bf16[4,64,1024]{2,1,0:T(8,128)(2,1)} %get-tuple-element.13.refs_1_, ...), custom_call_target="tpu_custom_call" | custom-call | tf_op jit(solution)/shard_map/pallas_call | solution.py:634

commit v14 on v13

--- a/solution.py
+++ b/solution.py
@@ -138,7 +138,7 @@
         if part == 0:
             bent = edge[d] & (s == 1)
         elif phase == 0:
-            bent = edge[d] & (s != d) & (g > 0)
+            bent = edge[d] & (s != d) & (g > 1)
             starts = starts & jnp.logical_not(skipped[d])
         else:
             bent = edge[d]
@@ -193,7 +193,7 @@
 
     def relays(g, phase):
         if phase == 0:
-            return is_relay & ((relay_column == 3) | ((relay_column == 2 - relay_back) & (g > 0)))
+            return is_relay & ((relay_column == 3) | ((relay_column == 2 - relay_back) & (g > 1)))
         return is_relay
 
     def slant_copy(g, d):
@@ -462,6 +462,7 @@
                 @pl.when(g == 0)
                 def _():
                     forward(1)
+                    relay_step(1, 0)
                     begin_keys(3)
                     begin_queries(2)
 
@@ -477,7 +478,6 @@
                 @pl.when(g == 0)
                 def _():
                     begin_queries(3)
-                    relay_step(1, 0)
 
                 @pl.when(g + 2 < GROUPS)
                 def _():

time: 74.5 us -> 76 us (1.020)
  Pallas kernels: 73.3 us -> 74.2 us
    pallas_call x1, Pallas kernels: 70.7 us -> 71.7 us  [body(): pl.pallas_call(lambda *refs: kernel(frames, *refs), out_shape=[shape] * 4...]
where the time goes in v14:
time: 76 us; the launch traced here: 74.9 us
  Pallas kernels  74.2 us (98%)
    pallas_call x1, Pallas kernels, body(): pl.pallas_call(lambda *refs: kernel(frames, *refs), out_shape=[shape] * 4...  71.7 us
    pallas_call x1, Pallas kernels, body(): pl.pallas_call(hand_over, out_shape=[shape] * 4, in_specs=[pl.BlockSpec(m...  2.57 us

profile of v14, /device:TPU:56, one launch (start us, length us, event | category | flops | bytes accessed | tf_op | source)
XLA Modules:
  0.0 74.9 jit_solution(13721748783963438221)
XLA Ops:
  0.6 71.7 %shard_map.93 = (bf16[4,64,1024]{2,1,0:T(8,128)(2,1)}, bf16[4,64,1024]{2,1,0:T(8,128)(2,1)}, bf16[4,64,1024]{2,1,0:T(8,128)(2,1)}, bf16[4,64,1024]{2,1,0:T(8,128)(2,1)}) custom-call(s32[4,13]{1,0:T(4,128)} %refs_0_.1, s32[4]{0:T(128)} %refs_1_.1, bf16[4,64,1024]{2,1,0:T(8,128)(2,1)} %bitcast.8, bf16[4,64,1024]{2,1,0:T(8,128)(2,1)} %bitcast.9, ...), custom_call_target="tpu_custom_call" | custom-call | flops 20937965568 | bytes 4194304 | tf_op jit(solution)/shard_map/pallas_call | solution.py:597
  72.3 2.6 %shard_map.94 = (bf16[4,64,1024]{2,1,0:T(8,128)(2,1)}, bf16[4,64,1024]{2,1,0:T(8,128)(2,1)}, bf16[4,64,1024]{2,1,0:T(8,128)(2,1)}, bf16[4,64,1024]{2,1,0:T(8,128)(2,1)}) custom-call(bf16[4,64,1024]{2,1,0:T(8,128)(2,1)} %get-tuple-element.12.refs_0_, bf16[4,64,1024]{2,1,0:T(8,128)(2,1)} %get-tuple-element.13.refs_1_, ...), custom_call_target="tpu_custom_call" | custom-call | tf_op jit(solution)/shard_map/pallas_call | solution.py:634

commit v15 on v13

--- a/solution.py
+++ b/solution.py
@@ -511,9 +511,9 @@
             give[g, 0, w] = gather(w, 2 * FRAME).astype(jnp.bfloat16)
             return inner
 
-        lax.fori_loop(0, FRAME, collect, 0)
-        for d in range(2):
-            for part in range(2):
+        for part, half in ((1, o), (0, s)):
+            lax.fori_loop(HALF * half, HALF * half + HALF, collect, 0)
+            for d in range(2):
                 start_terms(g, d, part)
 
         def collect_own(w, inner):

time: 74.5 us -> 74.4 us (level)
  no operation moved by 1% of the time
where the time goes in v15:
time: 74.4 us; the launch traced here: 73.8 us
  Pallas kernels  73.2 us (98%)
    pallas_call x1, Pallas kernels, body(): pl.pallas_call(lambda *refs: kernel(frames, *refs), out_shape=[shape] * 4...  70.6 us
    pallas_call x1, Pallas kernels, body(): pl.pallas_call(hand_over, out_shape=[shape] * 4, in_specs=[pl.BlockSpec(m...  2.57 us

profile of v15, /device:TPU:56, one launch (start us, length us, event | category | flops | bytes accessed | tf_op | source)
XLA Modules:
  0.0 73.8 jit_solution(11898502059706035477)
XLA Ops:
  0.6 70.6 %shard_map.93 = (bf16[4,64,1024]{2,1,0:T(8,128)(2,1)}, bf16[4,64,1024]{2,1,0:T(8,128)(2,1)}, bf16[4,64,1024]{2,1,0:T(8,128)(2,1)}, bf16[4,64,1024]{2,1,0:T(8,128)(2,1)}) custom-call(s32[4,13]{1,0:T(4,128)} %refs_0_.1, s32[4]{0:T(128)} %refs_1_.1, bf16[4,64,1024]{2,1,0:T(8,128)(2,1)} %bitcast.8, bf16[4,64,1024]{2,1,0:T(8,128)(2,1)} %bitcast.9, ...), custom_call_target="tpu_custom_call" | custom-call | flops 20937965568 | bytes 4194304 | tf_op jit(solution)/shard_map/pallas_call | solution.py:597
  71.3 2.6 %shard_map.94 = (bf16[4,64,1024]{2,1,0:T(8,128)(2,1)}, bf16[4,64,1024]{2,1,0:T(8,128)(2,1)}, bf16[4,64,1024]{2,1,0:T(8,128)(2,1)}, bf16[4,64,1024]{2,1,0:T(8,128)(2,1)}) custom-call(bf16[4,64,1024]{2,1,0:T(8,128)(2,1)} %get-tuple-element.12.refs_0_, bf16[4,64,1024]{2,1,0:T(8,128)(2,1)} %get-tuple-element.13.refs_1_, ...), custom_call_target="tpu_custom_call" | custom-call | tf_op jit(solution)/shard_map/pallas_call | solution.py:634
